TPU v7x, 512 devices: a whole 4x8x8 slice. The times are simulated.
512 devices in a mesh: row: 64 (over y, z_hi, core), col: 8 (over x, z_lo).
Axes of the slice: x: 4, y: 8, z: 8 (z_hi: 4, z_lo: 2; z = z_hi * 2 + z_lo), core: 2. Of those that a mesh axis runs over, the one named last changes fastest.
Arguments:
- panel_u: bfloat16 [64, 128, 2688], P('row', None, 'col'), may hold values from -0.115727512 to 0.115727512
- panel_v: bfloat16 [64, 128, 2688], P('row', None, 'col'), may hold values from -0.07324219 to 0.07324219
- panel_rank: int32 [64], P('row'), may hold values from 1 to 128
- trail_x: bfloat16 [512, 128, 2688], P('row', None, 'col'), may hold values from -6 to 6
- trail_y: bfloat16 [512, 128, 2688], P('row', None, 'col'), may hold values from -6 to 6
- trail_rank: int32 [512], P('row'), may hold values from 1 to 128
- tile_cols: int32 [512], P('row'), may hold values from 0 to 63
- owner: int32 [512, 1], P('row'), may hold values from 0 to 7; in each aligned block of 8 rows (0 to 7, 8 to 15, ...) at most 2 rows name the same one
Outputs:
- left_own: float32 [1024, 128, 128], P(('row', 'col'))
- left_cross: float32 [1024, 128, 128], P(('row', 'col'))
- left_new: float32 [1024, 128, 128], P(('row', 'col'))
- right_own: float32 [1024, 128, 128], P(('row', 'col'))
- right_cross: float32 [1024, 128, 128], P(('row', 'col'))
Inputs may be any that keep to these rules, and one draw needn't show every extreme that they name: Among the 8 trailing tiles of one grid row no owner holds more than 2.
All inputs are finite; a program needn't handle non-finite values.
Results may differ from a plain program's by a relative error of at most 0.0003.
Values may be sent and summed in bfloat16 or wider, within the bound.
No kernel may reach another device: no remote copies, remote signals or barrier semaphores. Data moves between devices by JAX's collectives and lax.ppermute only.
A program may use at most 128 MiB of HBM per device.

v0:
```python
import jax
import jax.numpy as jnp
from jax import lax
from jax.sharding import PartitionSpec as P


def shifted(shard, axis, by):
    length = lax.axis_size(axis)
    return lax.ppermute(shard, axis, [(i, (i + by) % length) for i in range(length)])


def clear_rows(factor, rank_list):
    kept_mask = lax.broadcasted_iota(jnp.int32, factor.shape, 1) < rank_list[:, None, None]
    return jnp.where(kept_mask, factor, jnp.zeros_like(factor))


def pair_product(first, second):
    return jnp.einsum("tks,tls->tkl", first, second, preferred_element_type=jnp.float32)


def select_tiles(chosen, terms):
    return tuple(
        (jnp.einsum("st,tkl->skl", chosen, term, precision=lax.Precision.HIGHEST) for term in terms)
    )


def per_device(panel_u, panel_v, panel_rank, trail_x, trail_y, trail_rank, tile_cols, owner):
    highest = lax.Precision.HIGHEST
    both_kept = jnp.stack([clear_rows(panel_u, panel_rank), clear_rows(panel_v, panel_rank)])
    kept_x = clear_rows(trail_x, trail_rank)
    kept_y = clear_rows(trail_y, trail_rank)
    own_left = pair_product(kept_x, kept_x)
    own_right = pair_product(kept_y, kept_y)
    tiles = trail_x.shape[0]
    left_here = both_kept[0, 0]
    right_here = both_kept[1, 0]
    gram_one = jnp.dot(left_here, left_here.T, preferred_element_type=jnp.float32)
    gram = jnp.broadcast_to(gram_one[None], (tiles,) + gram_one.shape)
    part_left = jnp.einsum("tks,ls->tkl", kept_x, left_here, preferred_element_type=jnp.float32)
    rows_here = panel_u.shape[0]
    cycle_size = lax.axis_size("row")
    own_index = lax.axis_index("row")
    stacked = jnp.zeros((2, cycle_size * rows_here) + panel_u.shape[1:], panel_u.dtype)

    def store_piece(turn_count, stacked, piece):
        source = (own_index - turn_count) % cycle_size
        return lax.dynamic_update_slice_in_dim(stacked, piece, source * rows_here, 1)

    stacked = store_piece(0, stacked, both_kept)

    def advance(turn_count, carried):
        stacked, piece = carried
        piece = shifted(piece, "row", 1)
        return (store_piece(turn_count, stacked, piece), piece)

    stacked, last_piece = lax.fori_loop(1, cycle_size, advance, (stacked, both_kept))
    left_j = jnp.take(stacked[0], tile_cols, axis=0)
    right_j = jnp.take(stacked[1], tile_cols, axis=0)
    core = jnp.einsum("ks,tls->tkl", right_here, right_j, preferred_element_type=jnp.float32)
    part_right = pair_product(kept_y, left_j)
    col_count = lax.axis_size("col")
    capacity = max(2, 2 * tiles // col_count)
    owners = owner[:, 0]
    order = lax.broadcasted_iota(jnp.int32, (tiles, tiles), 1)
    later = lax.broadcasted_iota(jnp.int32, (tiles, tiles), 0)
    before = (owners[None, :] == owners[:, None]) & (order < later)
    place_in = jnp.sum(before.astype(jnp.int32), axis=1)
    summed = lax.psum((core, gram, part_left, part_right, own_left, own_right), "col")
    column_here = lax.axis_index("col")
    slot_index = lax.broadcasted_iota(jnp.int32, (capacity, tiles), 0)
    chosen = ((owners[None, :] == column_here) & (place_in[None, :] == slot_index)).astype(
        jnp.float32
    )
    owned = select_tiles(chosen, summed)
    core_owned, gram_owned, left_owned, right_owned, own_left_owned, own_right_owned = owned
    left_cross = jnp.einsum("skl,slm->skm", left_owned, core_owned, precision=highest)
    inner = jnp.einsum("skl,slm->skm", gram_owned, core_owned, precision=highest)
    left_new = jnp.einsum("slk,slm->skm", core_owned, inner, precision=highest)
    return (own_left_owned, left_cross, left_new, own_right_owned, -right_owned)


def solution(mesh):
    placed = (
        P("row", None, "col"),
        P("row", None, "col"),
        P("row"),
        P("row", None, "col"),
        P("row", None, "col"),
        P("row"),
        P("row"),
        P("row", None),
    )
    return jax.shard_map(
        per_device,
        mesh=mesh,
        in_specs=placed,
        out_specs=(
            P(("row", "col"), None, None),
            P(("row", "col"), None, None),
            P(("row", "col"), None, None),
            P(("row", "col"), None, None),
            P(("row", "col"), None, None),
        ),
        check_vma=False,
    )
```

profile of v0, /device:TPU:1, one launch (start us, length us, event | category | flops | bytes accessed | tf_op | source)
XLA Modules:
  0.0 1021.5 jit_solution(14421400043011111308)
XLA Ops:
  18.6 799.1 %while.17 = (s32[]{:T(128)}, bf16[2,64,128,336]{3,2,1,0:T(8,128)(2,1)}, bf16[2,1,128,336]{3,2,1,0:T(8,128)(2,1)S(1)}, s32[]{:T(128)}, s32[]{:T(128)}, /*index=5*/s32[]{:T(128)}, s32[]{:T(128)}, s32[]{:T(128)}) while((s32[]{:T(128)}, bf16[2,64,128,336]{3,2,1,0:T(8,128)(2,1)}, bf16[2,1,128,336]{3,2,1,0:T(8,128)(2,1)S(1)}, s32[]{:T(128)}, ...), condition=%wide.region_4.5_spmd, body=%wide.region_3.4_spmd.sunk | while | flops 17 | bytes 1401116 | solution.py:56
  45.1 11.0 %collective-permute-done = bf16[2,1,128,336]{3,2,1,0:T(8,128)(2,1)S(1)} collective-permute-done((bf16[2,1,128,336]{3,2,1,0:T(8,128)(2,1)S(1)}, bf16[2,1,128,336]{3,2,1,0:T(8,128)(2,1)S(1)}, u32[]{:S(2)}, u32[]{:S(2)}) %collective-permute-start) | collective-permute-done | bytes 172064 | tf_op jit(solution)/shard_map/while/body/eval_jaxpr/ppermute | solution.py:9
  58.8 10.8 %collective-permute-done = bf16[2,1,128,336]{3,2,1,0:T(8,128)(2,1)S(1)} collective-permute-done((bf16[2,1,128,336]{3,2,1,0:T(8,128)(2,1)S(1)}, bf16[2,1,128,336]{3,2,1,0:T(8,128)(2,1)S(1)}, u32[]{:S(2)}, u32[]{:S(2)}) %collective-permute-start) | collective-permute-done | bytes 172064 | tf_op jit(solution)/shard_map/while/body/eval_jaxpr/ppermute | solution.py:9
  72.3 10.5 %collective-permute-done = bf16[2,1,128,336]{3,2,1,0:T(8,128)(2,1)S(1)} collective-permute-done((bf16[2,1,128,336]{3,2,1,0:T(8,128)(2,1)S(1)}, bf16[2,1,128,336]{3,2,1,0:T(8,128)(2,1)S(1)}, u32[]{:S(2)}, u32[]{:S(2)}) %collective-permute-start) | collective-permute-done | bytes 172064 | tf_op jit(solution)/shard_map/while/body/eval_jaxpr/ppermute | solution.py:9
  85.5 10.4 %collective-permute-done = bf16[2,1,128,336]{3,2,1,0:T(8,128)(2,1)S(1)} collective-permute-done((bf16[2,1,128,336]{3,2,1,0:T(8,128)(2,1)S(1)}, bf16[2,1,128,336]{3,2,1,0:T(8,128)(2,1)S(1)}, u32[]{:S(2)}, u32[]{:S(2)}) %collective-permute-start) | collective-permute-done | bytes 172064 | tf_op jit(solution)/shard_map/while/body/eval_jaxpr/ppermute | solution.py:9
  98.6 10.4 %collective-permute-done = bf16[2,1,128,336]{3,2,1,0:T(8,128)(2,1)S(1)} collective-permute-done((bf16[2,1,128,336]{3,2,1,0:T(8,128)(2,1)S(1)}, bf16[2,1,128,336]{3,2,1,0:T(8,128)(2,1)S(1)}, u32[]{:S(2)}, u32[]{:S(2)}) %collective-permute-start) | collective-permute-done | bytes 172064 | tf_op jit(solution)/shard_map/while/body/eval_jaxpr/ppermute | solution.py:9
  111.6 10.4 %collective-permute-done = bf16[2,1,128,336]{3,2,1,0:T(8,128)(2,1)S(1)} collective-permute-done((bf16[2,1,128,336]{3,2,1,0:T(8,128)(2,1)S(1)}, bf16[2,1,128,336]{3,2,1,0:T(8,128)(2,1)S(1)}, u32[]{:S(2)}, u32[]{:S(2)}) %collective-permute-start) | collective-permute-done | bytes 172064 | tf_op jit(solution)/shard_map/while/body/eval_jaxpr/ppermute | solution.py:9
  124.7 10.3 %collective-permute-done = bf16[2,1,128,336]{3,2,1,0:T(8,128)(2,1)S(1)} collective-permute-done((bf16[2,1,128,336]{3,2,1,0:T(8,128)(2,1)S(1)}, bf16[2,1,128,336]{3,2,1,0:T(8,128)(2,1)S(1)}, u32[]{:S(2)}, u32[]{:S(2)}) %collective-permute-start) | collective-permute-done | bytes 172064 | tf_op jit(solution)/shard_map/while/body/eval_jaxpr/ppermute | solution.py:9
  137.7 10.3 %collective-permute-done = bf16[2,1,128,336]{3,2,1,0:T(8,128)(2,1)S(1)} collective-permute-done((bf16[2,1,128,336]{3,2,1,0:T(8,128)(2,1)S(1)}, bf16[2,1,128,336]{3,2,1,0:T(8,128)(2,1)S(1)}, u32[]{:S(2)}, u32[]{:S(2)}) %collective-permute-start) | collective-permute-done | bytes 172064 | tf_op jit(solution)/shard_map/while/body/eval_jaxpr/ppermute | solution.py:9
  150.7 10.3 %collective-permute-done = bf16[2,1,128,336]{3,2,1,0:T(8,128)(2,1)S(1)} collective-permute-done((bf16[2,1,128,336]{3,2,1,0:T(8,128)(2,1)S(1)}, bf16[2,1,128,336]{3,2,1,0:T(8,128)(2,1)S(1)}, u32[]{:S(2)}, u32[]{:S(2)}) %collective-permute-start) | collective-permute-done | bytes 172064 | tf_op jit(solution)/shard_map/while/body/eval_jaxpr/ppermute | solution.py:9
  163.6 10.4 %collective-permute-done = bf16[2,1,128,336]{3,2,1,0:T(8,128)(2,1)S(1)} collective-permute-done((bf16[2,1,128,336]{3,2,1,0:T(8,128)(2,1)S(1)}, bf16[2,1,128,336]{3,2,1,0:T(8,128)(2,1)S(1)}, u32[]{:S(2)}, u32[]{:S(2)}) %collective-permute-start) | collective-permute-done | bytes 172064 | tf_op jit(solution)/shard_map/while/body/eval_jaxpr/ppermute | solution.py:9
  176.7 10.7 %collective-permute-done = bf16[2,1,128,336]{3,2,1,0:T(8,128)(2,1)S(1)} collective-permute-done((bf16[2,1,128,336]{3,2,1,0:T(8,128)(2,1)S(1)}, bf16[2,1,128,336]{3,2,1,0:T(8,128)(2,1)S(1)}, u32[]{:S(2)}, u32[]{:S(2)}) %collective-permute-start) | collective-permute-done | bytes 172064 | tf_op jit(solution)/shard_map/while/body/eval_jaxpr/ppermute | solution.py:9
  190.1 10.6 %collective-permute-done = bf16[2,1,128,336]{3,2,1,0:T(8,128)(2,1)S(1)} collective-permute-done((bf16[2,1,128,336]{3,2,1,0:T(8,128)(2,1)S(1)}, bf16[2,1,128,336]{3,2,1,0:T(8,128)(2,1)S(1)}, u32[]{:S(2)}, u32[]{:S(2)}) %collective-permute-start) | collective-permute-done | bytes 172064 | tf_op jit(solution)/shard_map/while/body/eval_jaxpr/ppermute | solution.py:9
  288.1 9.9 collective-permute-done
  300.7 10.5 %collective-permute-done = bf16[2,1,128,336]{3,2,1,0:T(8,128)(2,1)S(1)} collective-permute-done((bf16[2,1,128,336]{3,2,1,0:T(8,128)(2,1)S(1)}, bf16[2,1,128,336]{3,2,1,0:T(8,128)(2,1)S(1)}, u32[]{:S(2)}, u32[]{:S(2)}) %collective-permute-start) | collective-permute-done | bytes 172064 | tf_op jit(solution)/shard_map/while/body/eval_jaxpr/ppermute | solution.py:9
  313.9 10.6 %collective-permute-done = bf16[2,1,128,336]{3,2,1,0:T(8,128)(2,1)S(1)} collective-permute-done((bf16[2,1,128,336]{3,2,1,0:T(8,128)(2,1)S(1)}, bf16[2,1,128,336]{3,2,1,0:T(8,128)(2,1)S(1)}, u32[]{:S(2)}, u32[]{:S(2)}) %collective-permute-start) | collective-permute-done | bytes 172064 | tf_op jit(solution)/shard_map/while/body/eval_jaxpr/ppermute | solution.py:9
  351.6 10.0 collective-permute-done
  364.3 10.5 %collective-permute-done = bf16[2,1,128,336]{3,2,1,0:T(8,128)(2,1)S(1)} collective-permute-done((bf16[2,1,128,336]{3,2,1,0:T(8,128)(2,1)S(1)}, bf16[2,1,128,336]{3,2,1,0:T(8,128)(2,1)S(1)}, u32[]{:S(2)}, u32[]{:S(2)}) %collective-permute-start) | collective-permute-done | bytes 172064 | tf_op jit(solution)/shard_map/while/body/eval_jaxpr/ppermute | solution.py:9
  389.4 10.1 collective-permute-done
  402.2 9.8 collective-permute-done
  623.3 9.9 collective-permute-done
  635.9 10.7 %collective-permute-done = bf16[2,1,128,336]{3,2,1,0:T(8,128)(2,1)S(1)} collective-permute-done((bf16[2,1,128,336]{3,2,1,0:T(8,128)(2,1)S(1)}, bf16[2,1,128,336]{3,2,1,0:T(8,128)(2,1)S(1)}, u32[]{:S(2)}, u32[]{:S(2)}) %collective-permute-start) | collective-permute-done | bytes 172064 | tf_op jit(solution)/shard_map/while/body/eval_jaxpr/ppermute | solution.py:9
  649.3 11.6 %collective-permute-done = bf16[2,1,128,336]{3,2,1,0:T(8,128)(2,1)S(1)} collective-permute-done((bf16[2,1,128,336]{3,2,1,0:T(8,128)(2,1)S(1)}, bf16[2,1,128,336]{3,2,1,0:T(8,128)(2,1)S(1)}, u32[]{:S(2)}, u32[]{:S(2)}) %collective-permute-start) | collective-permute-done | bytes 172064 | tf_op jit(solution)/shard_map/while/body/eval_jaxpr/ppermute | solution.py:9
  663.6 11.5 %collective-permute-done = bf16[2,1,128,336]{3,2,1,0:T(8,128)(2,1)S(1)} collective-permute-done((bf16[2,1,128,336]{3,2,1,0:T(8,128)(2,1)S(1)}, bf16[2,1,128,336]{3,2,1,0:T(8,128)(2,1)S(1)}, u32[]{:S(2)}, u32[]{:S(2)}) %collective-permute-start) | collective-permute-done | bytes 172064 | tf_op jit(solution)/shard_map/while/body/eval_jaxpr/ppermute | solution.py:9
  677.7 11.2 %collective-permute-done = bf16[2,1,128,336]{3,2,1,0:T(8,128)(2,1)S(1)} collective-permute-done((bf16[2,1,128,336]{3,2,1,0:T(8,128)(2,1)S(1)}, bf16[2,1,128,336]{3,2,1,0:T(8,128)(2,1)S(1)}, u32[]{:S(2)}, u32[]{:S(2)}) %collective-permute-start) | collective-permute-done | bytes 172064 | tf_op jit(solution)/shard_map/while/body/eval_jaxpr/ppermute | solution.py:9
  691.6 10.8 %collective-permute-done = bf16[2,1,128,336]{3,2,1,0:T(8,128)(2,1)S(1)} collective-permute-done((bf16[2,1,128,336]{3,2,1,0:T(8,128)(2,1)S(1)}, bf16[2,1,128,336]{3,2,1,0:T(8,128)(2,1)S(1)}, u32[]{:S(2)}, u32[]{:S(2)}) %collective-permute-start) | collective-permute-done | bytes 172064 | tf_op jit(solution)/shard_map/while/body/eval_jaxpr/ppermute | solution.py:9
  705.1 10.7 %collective-permute-done = bf16[2,1,128,336]{3,2,1,0:T(8,128)(2,1)S(1)} collective-permute-done((bf16[2,1,128,336]{3,2,1,0:T(8,128)(2,1)S(1)}, bf16[2,1,128,336]{3,2,1,0:T(8,128)(2,1)S(1)}, u32[]{:S(2)}, u32[]{:S(2)}) %collective-permute-start) | collective-permute-done | bytes 172064 | tf_op jit(solution)/shard_map/while/body/eval_jaxpr/ppermute | solution.py:9
  718.4 10.5 %collective-permute-done = bf16[2,1,128,336]{3,2,1,0:T(8,128)(2,1)S(1)} collective-permute-done((bf16[2,1,128,336]{3,2,1,0:T(8,128)(2,1)S(1)}, bf16[2,1,128,336]{3,2,1,0:T(8,128)(2,1)S(1)}, u32[]{:S(2)}, u32[]{:S(2)}) %collective-permute-start) | collective-permute-done | bytes 172064 | tf_op jit(solution)/shard_map/while/body/eval_jaxpr/ppermute | solution.py:9
  731.6 10.7 %collective-permute-done = bf16[2,1,128,336]{3,2,1,0:T(8,128)(2,1)S(1)} collective-permute-done((bf16[2,1,128,336]{3,2,1,0:T(8,128)(2,1)S(1)}, bf16[2,1,128,336]{3,2,1,0:T(8,128)(2,1)S(1)}, u32[]{:S(2)}, u32[]{:S(2)}) %collective-permute-start) | collective-permute-done | bytes 172064 | tf_op jit(solution)/shard_map/while/body/eval_jaxpr/ppermute | solution.py:9
  782.2 9.8 collective-permute-done
  817.7 10.8 %slice_bitcast_fusion = (bf16[64,128,336]{2,1,0:T(8,128)(2,1)}, bf16[64,128,336]{2,1,0:T(8,128)(2,1)}) fusion(bf16[2,64,128,336]{3,2,1,0:T(8,128)(2,1)} %get-tuple-element.117), kind=kLoop, calls=%fused_computation.3 | loop fusion | bytes 22020096 | tf_op jit(solution)/shard_map/squeeze | solution.py:57
  844.9 156.3 %all-reduce.3.cloned.1.call-done = (f32[8,128,128]{2,0,1:T(8,128)}, f32[8,128,128]{2,0,1:T(8,128)}, f32[8,128,128]{2,1,0:T(8,128)}, f32[8,128,128]{2,1,0:T(8,128...) async-done(((f32[8,128,128]{2,0,1:T(8,128)}, f32[8,128,128]{2,0,1:T(8,128)}, f32[8,128,128]{2,1,0:T(8,128)}, f32[8,128,128]{2,1,0:T(8,128)}, f32[8,128,128]{2,0,1:T(8,128)}, ...) | async-done | bytes 3145744 | tf_op jit(solution)/shard_map/psum | solution.py:68
  (270 shorter events, 532.2 us)
Async XLA Ops:
  7.2 994.0 %all-reduce.3.cloned.1.call-start = ((), (), s32[]{:S(2)}) async-start(), calls=%async_computation | async-start | bytes 6291456 | tf_op jit(solution)/shard_map/psum | solution.py:68
  29.2 13.3 %collective-permute-start = (bf16[2,1,128,336]{3,2,1,0:T(8,128)(2,1)S(1)}, bf16[2,1,128,336]{3,2,1,0:T(8,128)(2,1)S(1)}, u32[]{:S(2)}, u32[]{:S(2)}) collective-permute-start(bf16[2,1,128,336]{3,2,1,0:T(8,128)(2,1)S(1)} %get-tuple-element.183), channel_id=1, source_target_pairs={{0,8},{8,16},{16,24},{24,32},{32,40},{40,48},{48,56},{56,64},{64,7... | collective-permute-start | bytes 516104 | tf_op jit(solution)/shard_map/while/body/eval_jaxpr/ppermute | solution.py:9
  43.2 12.9 %collective-permute-start = (bf16[2,1,128,336]{3,2,1,0:T(8,128)(2,1)S(1)}, bf16[2,1,128,336]{3,2,1,0:T(8,128)(2,1)S(1)}, u32[]{:S(2)}, u32[]{:S(2)}) collective-permute-start(bf16[2,1,128,336]{3,2,1,0:T(8,128)(2,1)S(1)} %get-tuple-element.183), channel_id=1, source_target_pairs={{0,8},{8,16},{16,24},{24,32},{32,40},{40,48},{48,56},{56,64},{64,7... | collective-permute-start | bytes 516104 | tf_op jit(solution)/shard_map/while/body/eval_jaxpr/ppermute | solution.py:9
  56.9 12.7 %collective-permute-start = (bf16[2,1,128,336]{3,2,1,0:T(8,128)(2,1)S(1)}, bf16[2,1,128,336]{3,2,1,0:T(8,128)(2,1)S(1)}, u32[]{:S(2)}, u32[]{:S(2)}) collective-permute-start(bf16[2,1,128,336]{3,2,1,0:T(8,128)(2,1)S(1)} %get-tuple-element.183), channel_id=1, source_target_pairs={{0,8},{8,16},{16,24},{24,32},{32,40},{40,48},{48,56},{56,64},{64,7... | collective-permute-start | bytes 516104 | tf_op jit(solution)/shard_map/while/body/eval_jaxpr/ppermute | solution.py:9
  70.3 12.5 %collective-permute-start = (bf16[2,1,128,336]{3,2,1,0:T(8,128)(2,1)S(1)}, bf16[2,1,128,336]{3,2,1,0:T(8,128)(2,1)S(1)}, u32[]{:S(2)}, u32[]{:S(2)}) collective-permute-start(bf16[2,1,128,336]{3,2,1,0:T(8,128)(2,1)S(1)} %get-tuple-element.183), channel_id=1, source_target_pairs={{0,8},{8,16},{16,24},{24,32},{32,40},{40,48},{48,56},{56,64},{64,7... | collective-permute-start | bytes 516104 | tf_op jit(solution)/shard_map/while/body/eval_jaxpr/ppermute | solution.py:9
  83.5 12.4 %collective-permute-start = (bf16[2,1,128,336]{3,2,1,0:T(8,128)(2,1)S(1)}, bf16[2,1,128,336]{3,2,1,0:T(8,128)(2,1)S(1)}, u32[]{:S(2)}, u32[]{:S(2)}) collective-permute-start(bf16[2,1,128,336]{3,2,1,0:T(8,128)(2,1)S(1)} %get-tuple-element.183), channel_id=1, source_target_pairs={{0,8},{8,16},{16,24},{24,32},{32,40},{40,48},{48,56},{56,64},{64,7... | collective-permute-start | bytes 516104 | tf_op jit(solution)/shard_map/while/body/eval_jaxpr/ppermute | solution.py:9
  96.6 12.3 %collective-permute-start = (bf16[2,1,128,336]{3,2,1,0:T(8,128)(2,1)S(1)}, bf16[2,1,128,336]{3,2,1,0:T(8,128)(2,1)S(1)}, u32[]{:S(2)}, u32[]{:S(2)}) collective-permute-start(bf16[2,1,128,336]{3,2,1,0:T(8,128)(2,1)S(1)} %get-tuple-element.183), channel_id=1, source_target_pairs={{0,8},{8,16},{16,24},{24,32},{32,40},{40,48},{48,56},{56,64},{64,7... | collective-permute-start | bytes 516104 | tf_op jit(solution)/shard_map/while/body/eval_jaxpr/ppermute | solution.py:9
  109.7 12.3 %collective-permute-start = (bf16[2,1,128,336]{3,2,1,0:T(8,128)(2,1)S(1)}, bf16[2,1,128,336]{3,2,1,0:T(8,128)(2,1)S(1)}, u32[]{:S(2)}, u32[]{:S(2)}) collective-permute-start(bf16[2,1,128,336]{3,2,1,0:T(8,128)(2,1)S(1)} %get-tuple-element.183), channel_id=1, source_target_pairs={{0,8},{8,16},{16,24},{24,32},{32,40},{40,48},{48,56},{56,64},{64,7... | collective-permute-start | bytes 516104 | tf_op jit(solution)/shard_map/while/body/eval_jaxpr/ppermute | solution.py:9
  122.7 12.3 %collective-permute-start = (bf16[2,1,128,336]{3,2,1,0:T(8,128)(2,1)S(1)}, bf16[2,1,128,336]{3,2,1,0:T(8,128)(2,1)S(1)}, u32[]{:S(2)}, u32[]{:S(2)}) collective-permute-start(bf16[2,1,128,336]{3,2,1,0:T(8,128)(2,1)S(1)} %get-tuple-element.183), channel_id=1, source_target_pairs={{0,8},{8,16},{16,24},{24,32},{32,40},{40,48},{48,56},{56,64},{64,7... | collective-permute-start | bytes 516104 | tf_op jit(solution)/shard_map/while/body/eval_jaxpr/ppermute | solution.py:9
  135.7 12.2 %collective-permute-start = (bf16[2,1,128,336]{3,2,1,0:T(8,128)(2,1)S(1)}, bf16[2,1,128,336]{3,2,1,0:T(8,128)(2,1)S(1)}, u32[]{:S(2)}, u32[]{:S(2)}) collective-permute-start(bf16[2,1,128,336]{3,2,1,0:T(8,128)(2,1)S(1)} %get-tuple-element.183), channel_id=1, source_target_pairs={{0,8},{8,16},{16,24},{24,32},{32,40},{40,48},{48,56},{56,64},{64,7... | collective-permute-start | bytes 516104 | tf_op jit(solution)/shard_map/while/body/eval_jaxpr/ppermute | solution.py:9
  148.7 12.2 %collective-permute-start = (bf16[2,1,128,336]{3,2,1,0:T(8,128)(2,1)S(1)}, bf16[2,1,128,336]{3,2,1,0:T(8,128)(2,1)S(1)}, u32[]{:S(2)}, u32[]{:S(2)}) collective-permute-start(bf16[2,1,128,336]{3,2,1,0:T(8,128)(2,1)S(1)} %get-tuple-element.183), channel_id=1, source_target_pairs={{0,8},{8,16},{16,24},{24,32},{32,40},{40,48},{48,56},{56,64},{64,7... | collective-permute-start | bytes 516104 | tf_op jit(solution)/shard_map/while/body/eval_jaxpr/ppermute | solution.py:9
  161.7 12.3 %collective-permute-start = (bf16[2,1,128,336]{3,2,1,0:T(8,128)(2,1)S(1)}, bf16[2,1,128,336]{3,2,1,0:T(8,128)(2,1)S(1)}, u32[]{:S(2)}, u32[]{:S(2)}) collective-permute-start(bf16[2,1,128,336]{3,2,1,0:T(8,128)(2,1)S(1)} %get-tuple-element.183), channel_id=1, source_target_pairs={{0,8},{8,16},{16,24},{24,32},{32,40},{40,48},{48,56},{56,64},{64,7... | collective-permute-start | bytes 516104 | tf_op jit(solution)/shard_map/while/body/eval_jaxpr/ppermute | solution.py:9
  174.7 12.7 %collective-permute-start = (bf16[2,1,128,336]{3,2,1,0:T(8,128)(2,1)S(1)}, bf16[2,1,128,336]{3,2,1,0:T(8,128)(2,1)S(1)}, u32[]{:S(2)}, u32[]{:S(2)}) collective-permute-start(bf16[2,1,128,336]{3,2,1,0:T(8,128)(2,1)S(1)} %get-tuple-element.183), channel_id=1, source_target_pairs={{0,8},{8,16},{16,24},{24,32},{32,40},{40,48},{48,56},{56,64},{64,7... | collective-permute-start | bytes 516104 | tf_op jit(solution)/shard_map/while/body/eval_jaxpr/ppermute | solution.py:9
  188.1 12.5 %collective-permute-start = (bf16[2,1,128,336]{3,2,1,0:T(8,128)(2,1)S(1)}, bf16[2,1,128,336]{3,2,1,0:T(8,128)(2,1)S(1)}, u32[]{:S(2)}, u32[]{:S(2)}) collective-permute-start(bf16[2,1,128,336]{3,2,1,0:T(8,128)(2,1)S(1)} %get-tuple-element.183), channel_id=1, source_target_pairs={{0,8},{8,16},{16,24},{24,32},{32,40},{40,48},{48,56},{56,64},{64,7... | collective-permute-start | bytes 516104 | tf_op jit(solution)/shard_map/while/body/eval_jaxpr/ppermute | solution.py:9
  286.2 11.9 %collective-permute-start = (bf16[2,1,128,336]{3,2,1,0:T(8,128)(2,1)S(1)}, bf16[2,1,128,336]{3,2,1,0:T(8,128)(2,1)S(1)}, u32[]{:S(2)}, u32[]{:S(2)}) collective-permute-start(bf16[2,1,128,336]{3,2,1,0:T(8,128)(2,1)S(1)} %get-tuple-element.183), channel_id=1, source_target_pairs={{0,8},{8,16},{16,24},{24,32},{32,40},{40,48},{48,56},{56,64},{64,7... | collective-permute-start | bytes 516104 | tf_op jit(solution)/shard_map/while/body/eval_jaxpr/ppermute | solution.py:9
  298.8 12.4 %collective-permute-start = (bf16[2,1,128,336]{3,2,1,0:T(8,128)(2,1)S(1)}, bf16[2,1,128,336]{3,2,1,0:T(8,128)(2,1)S(1)}, u32[]{:S(2)}, u32[]{:S(2)}) collective-permute-start(bf16[2,1,128,336]{3,2,1,0:T(8,128)(2,1)S(1)} %get-tuple-element.183), channel_id=1, source_target_pairs={{0,8},{8,16},{16,24},{24,32},{32,40},{40,48},{48,56},{56,64},{64,7... | collective-permute-start | bytes 516104 | tf_op jit(solution)/shard_map/while/body/eval_jaxpr/ppermute | solution.py:9
  311.9 12.6 %collective-permute-start = (bf16[2,1,128,336]{3,2,1,0:T(8,128)(2,1)S(1)}, bf16[2,1,128,336]{3,2,1,0:T(8,128)(2,1)S(1)}, u32[]{:S(2)}, u32[]{:S(2)}) collective-permute-start(bf16[2,1,128,336]{3,2,1,0:T(8,128)(2,1)S(1)} %get-tuple-element.183), channel_id=1, source_target_pairs={{0,8},{8,16},{16,24},{24,32},{32,40},{40,48},{48,56},{56,64},{64,7... | collective-permute-start | bytes 516104 | tf_op jit(solution)/shard_map/while/body/eval_jaxpr/ppermute | solution.py:9
  349.7 11.9 %collective-permute-start = (bf16[2,1,128,336]{3,2,1,0:T(8,128)(2,1)S(1)}, bf16[2,1,128,336]{3,2,1,0:T(8,128)(2,1)S(1)}, u32[]{:S(2)}, u32[]{:S(2)}) collective-permute-start(bf16[2,1,128,336]{3,2,1,0:T(8,128)(2,1)S(1)} %get-tuple-element.183), channel_id=1, source_target_pairs={{0,8},{8,16},{16,24},{24,32},{32,40},{40,48},{48,56},{56,64},{64,7... | collective-permute-start | bytes 516104 | tf_op jit(solution)/shard_map/while/body/eval_jaxpr/ppermute | solution.py:9
  362.3 12.4 %collective-permute-start = (bf16[2,1,128,336]{3,2,1,0:T(8,128)(2,1)S(1)}, bf16[2,1,128,336]{3,2,1,0:T(8,128)(2,1)S(1)}, u32[]{:S(2)}, u32[]{:S(2)}) collective-permute-start(bf16[2,1,128,336]{3,2,1,0:T(8,128)(2,1)S(1)} %get-tuple-element.183), channel_id=1, source_target_pairs={{0,8},{8,16},{16,24},{24,32},{32,40},{40,48},{48,56},{56,64},{64,7... | collective-permute-start | bytes 516104 | tf_op jit(solution)/shard_map/while/body/eval_jaxpr/ppermute | solution.py:9
  387.4 12.1 %collective-permute-start = (bf16[2,1,128,336]{3,2,1,0:T(8,128)(2,1)S(1)}, bf16[2,1,128,336]{3,2,1,0:T(8,128)(2,1)S(1)}, u32[]{:S(2)}, u32[]{:S(2)}) collective-permute-start(bf16[2,1,128,336]{3,2,1,0:T(8,128)(2,1)S(1)} %get-tuple-element.183), channel_id=1, source_target_pairs={{0,8},{8,16},{16,24},{24,32},{32,40},{40,48},{48,56},{56,64},{64,7... | collective-permute-start | bytes 516104 | tf_op jit(solution)/shard_map/while/body/eval_jaxpr/ppermute | solution.py:9
  400.2 11.8 %collective-permute-start = (bf16[2,1,128,336]{3,2,1,0:T(8,128)(2,1)S(1)}, bf16[2,1,128,336]{3,2,1,0:T(8,128)(2,1)S(1)}, u32[]{:S(2)}, u32[]{:S(2)}) collective-permute-start(bf16[2,1,128,336]{3,2,1,0:T(8,128)(2,1)S(1)} %get-tuple-element.183), channel_id=1, source_target_pairs={{0,8},{8,16},{16,24},{24,32},{32,40},{40,48},{48,56},{56,64},{64,7... | collective-permute-start | bytes 516104 | tf_op jit(solution)/shard_map/while/body/eval_jaxpr/ppermute | solution.py:9
  621.4 11.8 %collective-permute-start = (bf16[2,1,128,336]{3,2,1,0:T(8,128)(2,1)S(1)}, bf16[2,1,128,336]{3,2,1,0:T(8,128)(2,1)S(1)}, u32[]{:S(2)}, u32[]{:S(2)}) collective-permute-start(bf16[2,1,128,336]{3,2,1,0:T(8,128)(2,1)S(1)} %get-tuple-element.183), channel_id=1, source_target_pairs={{0,8},{8,16},{16,24},{24,32},{32,40},{40,48},{48,56},{56,64},{64,7... | collective-permute-start | bytes 516104 | tf_op jit(solution)/shard_map/while/body/eval_jaxpr/ppermute | solution.py:9
  634.0 12.6 %collective-permute-start = (bf16[2,1,128,336]{3,2,1,0:T(8,128)(2,1)S(1)}, bf16[2,1,128,336]{3,2,1,0:T(8,128)(2,1)S(1)}, u32[]{:S(2)}, u32[]{:S(2)}) collective-permute-start(bf16[2,1,128,336]{3,2,1,0:T(8,128)(2,1)S(1)} %get-tuple-element.183), channel_id=1, source_target_pairs={{0,8},{8,16},{16,24},{24,32},{32,40},{40,48},{48,56},{56,64},{64,7... | collective-permute-start | bytes 516104 | tf_op jit(solution)/shard_map/while/body/eval_jaxpr/ppermute | solution.py:9
  647.3 13.6 %collective-permute-start = (bf16[2,1,128,336]{3,2,1,0:T(8,128)(2,1)S(1)}, bf16[2,1,128,336]{3,2,1,0:T(8,128)(2,1)S(1)}, u32[]{:S(2)}, u32[]{:S(2)}) collective-permute-start(bf16[2,1,128,336]{3,2,1,0:T(8,128)(2,1)S(1)} %get-tuple-element.183), channel_id=1, source_target_pairs={{0,8},{8,16},{16,24},{24,32},{32,40},{40,48},{48,56},{56,64},{64,7... | collective-permute-start | bytes 516104 | tf_op jit(solution)/shard_map/while/body/eval_jaxpr/ppermute | solution.py:9
  661.6 13.4 %collective-permute-start = (bf16[2,1,128,336]{3,2,1,0:T(8,128)(2,1)S(1)}, bf16[2,1,128,336]{3,2,1,0:T(8,128)(2,1)S(1)}, u32[]{:S(2)}, u32[]{:S(2)}) collective-permute-start(bf16[2,1,128,336]{3,2,1,0:T(8,128)(2,1)S(1)} %get-tuple-element.183), channel_id=1, source_target_pairs={{0,8},{8,16},{16,24},{24,32},{32,40},{40,48},{48,56},{56,64},{64,7... | collective-permute-start | bytes 516104 | tf_op jit(solution)/shard_map/while/body/eval_jaxpr/ppermute | solution.py:9
  675.8 13.1 %collective-permute-start = (bf16[2,1,128,336]{3,2,1,0:T(8,128)(2,1)S(1)}, bf16[2,1,128,336]{3,2,1,0:T(8,128)(2,1)S(1)}, u32[]{:S(2)}, u32[]{:S(2)}) collective-permute-start(bf16[2,1,128,336]{3,2,1,0:T(8,128)(2,1)S(1)} %get-tuple-element.183), channel_id=1, source_target_pairs={{0,8},{8,16},{16,24},{24,32},{32,40},{40,48},{48,56},{56,64},{64,7... | collective-permute-start | bytes 516104 | tf_op jit(solution)/shard_map/while/body/eval_jaxpr/ppermute | solution.py:9
  689.6 12.8 %collective-permute-start = (bf16[2,1,128,336]{3,2,1,0:T(8,128)(2,1)S(1)}, bf16[2,1,128,336]{3,2,1,0:T(8,128)(2,1)S(1)}, u32[]{:S(2)}, u32[]{:S(2)}) collective-permute-start(bf16[2,1,128,336]{3,2,1,0:T(8,128)(2,1)S(1)} %get-tuple-element.183), channel_id=1, source_target_pairs={{0,8},{8,16},{16,24},{24,32},{32,40},{40,48},{48,56},{56,64},{64,7... | collective-permute-start | bytes 516104 | tf_op jit(solution)/shard_map/while/body/eval_jaxpr/ppermute | solution.py:9
  703.1 12.6 %collective-permute-start = (bf16[2,1,128,336]{3,2,1,0:T(8,128)(2,1)S(1)}, bf16[2,1,128,336]{3,2,1,0:T(8,128)(2,1)S(1)}, u32[]{:S(2)}, u32[]{:S(2)}) collective-permute-start(bf16[2,1,128,336]{3,2,1,0:T(8,128)(2,1)S(1)} %get-tuple-element.183), channel_id=1, source_target_pairs={{0,8},{8,16},{16,24},{24,32},{32,40},{40,48},{48,56},{56,64},{64,7... | collective-permute-start | bytes 516104 | tf_op jit(solution)/shard_map/while/body/eval_jaxpr/ppermute | solution.py:9
  716.5 12.5 %collective-permute-start = (bf16[2,1,128,336]{3,2,1,0:T(8,128)(2,1)S(1)}, bf16[2,1,128,336]{3,2,1,0:T(8,128)(2,1)S(1)}, u32[]{:S(2)}, u32[]{:S(2)}) collective-permute-start(bf16[2,1,128,336]{3,2,1,0:T(8,128)(2,1)S(1)} %get-tuple-element.183), channel_id=1, source_target_pairs={{0,8},{8,16},{16,24},{24,32},{32,40},{40,48},{48,56},{56,64},{64,7... | collective-permute-start | bytes 516104 | tf_op jit(solution)/shard_map/while/body/eval_jaxpr/ppermute | solution.py:9
  729.7 12.6 %collective-permute-start = (bf16[2,1,128,336]{3,2,1,0:T(8,128)(2,1)S(1)}, bf16[2,1,128,336]{3,2,1,0:T(8,128)(2,1)S(1)}, u32[]{:S(2)}, u32[]{:S(2)}) collective-permute-start(bf16[2,1,128,336]{3,2,1,0:T(8,128)(2,1)S(1)} %get-tuple-element.183), channel_id=1, source_target_pairs={{0,8},{8,16},{16,24},{24,32},{32,40},{40,48},{48,56},{56,64},{64,7... | collective-permute-start | bytes 516104 | tf_op jit(solution)/shard_map/while/body/eval_jaxpr/ppermute | solution.py:9
  743.0 11.7 %collective-permute-start = (bf16[2,1,128,336]{3,2,1,0:T(8,128)(2,1)S(1)}, bf16[2,1,128,336]{3,2,1,0:T(8,128)(2,1)S(1)}, u32[]{:S(2)}, u32[]{:S(2)}) collective-permute-start(bf16[2,1,128,336]{3,2,1,0:T(8,128)(2,1)S(1)} %get-tuple-element.183), channel_id=1, source_target_pairs={{0,8},{8,16},{16,24},{24,32},{32,40},{40,48},{48,56},{56,64},{64,7... | collective-permute-start | bytes 516104 | tf_op jit(solution)/shard_map/while/body/eval_jaxpr/ppermute | solution.py:9
  780.3 11.8 %collective-permute-start = (bf16[2,1,128,336]{3,2,1,0:T(8,128)(2,1)S(1)}, bf16[2,1,128,336]{3,2,1,0:T(8,128)(2,1)S(1)}, u32[]{:S(2)}, u32[]{:S(2)}) collective-permute-start(bf16[2,1,128,336]{3,2,1,0:T(8,128)(2,1)S(1)} %get-tuple-element.183), channel_id=1, source_target_pairs={{0,8},{8,16},{16,24},{24,32},{32,40},{40,48},{48,56},{56,64},{64,7... | collective-permute-start | bytes 516104 | tf_op jit(solution)/shard_map/while/body/eval_jaxpr/ppermute | solution.py:9
  (36 other events, 423.4 us)
Sparse Core Ops, SparseCore 0:
  844.8 156.3 all-reduce.2
where the time goes:
time: 1020 us
  waiting for transfers between devices  778 us (76%)
  starting transfers between devices  129 us (13%)
  local copies, waits for them, and re-layouts  79.9 us (8%)
  matrix products  15.1 us (1%)
  between operations  14.9 us (1%)
    ppermute x63, waiting for transfers between devices, shifted(): lax.ppermute(shard, axis, [(i, (i + by) % length) for i in range(length)])  622 us
    psum x1, waiting for transfers between devices, per_device(): lax.psum((core, gram, part_left, part_right, own_left, own_right), 'col')  156 us
    ppermute x63, starting transfers between devices, shifted(): lax.ppermute(shard, axis, [(i, (i + by) % length) for i in range(length)])  129 us
    dynamic_update_slice x63, local copies, waits for them, and re-layouts, store_piece(): lax.dynamic_update_slice_in_dim(stacked, piece, source * rows_here, 1)  44.8 us
  transfers between devices with their start and end apart: 64, of which 64 were waited for; matrix products, arithmetic and copies ran while one was open for 0% of the time, Pallas kernels for 0%

commit v1 on v0

v1 whole, which is shorter than its diff:
```python
import jax
import jax.numpy as jnp
from jax import lax
from jax.experimental import pallas as pl
from jax.experimental.pallas import tpu as pltpu
from jax.sharding import PartitionSpec as P

K = 128
S = 336
TILES = 8
PEERS = 64
COLS = 8
FULL = 10
HALF = K // 2
WIDE = (FULL + 1) * K
EARLY = 5 * K + 8
SPLIT = S - 16


def tile_dot(first, second):
    return lax.dot_general(
        first, second, (((0,), (0,)), ((), ())), preferred_element_type=jnp.float32
    )


def exact_dot(first, second, lhs_dim=1):
    return lax.dot_general(
        first,
        second,
        (((lhs_dim,), (0,)), ((), ())),
        precision=lax.Precision.HIGHEST,
        preferred_element_type=jnp.float32,
    )


def keep(block, rank):
    lane = lax.broadcasted_iota(jnp.int32, block.shape, block.ndim - 1)
    return jnp.where(lane < rank, block, jnp.zeros_like(block))


def owned_tiles(owner_ref, column):
    first = jnp.int32(-1)
    second = jnp.int32(-1)
    for t in range(TILES):
        mine = owner_ref[t] == column
        second = jnp.where(mine & (first >= 0), t, second)
        first = jnp.where(mine & (first < 0), t, first)
    return first, second


def early_kernel(owner_ref, rank_ref, panel_rank_ref, x_ref, y_ref, u_ref, out_ref, gram_ref):
    column = pl.program_id(0)
    left = keep(u_ref[...], panel_rank_ref[0])

    @pl.when(column == 0)
    def _():
        gram_ref[...] = tile_dot(left, left)

    row_at = lax.broadcasted_iota(jnp.int32, (K, K), 0)
    col_at = lax.broadcasted_iota(jnp.int32, (K, K), 1)
    out_ref[0, 4 * K : 5 * K, :] = gram_ref[...]
    out_ref[0, 5 * K : EARLY, :] = jnp.zeros((EARLY - 5 * K, K), jnp.float32)
    for place, t in enumerate(owned_tiles(owner_ref, column)):
        base = 2 * place * K

        @pl.when(t >= 0)
        def _():
            x = keep(x_ref[t], rank_ref[t])
            y = keep(y_ref[t], rank_ref[t])
            both = tile_dot(x, jnp.concatenate([x, left], axis=1))
            right = tile_dot(y, y)
            out_ref[0, base : base + K, :] = both[:, K:]
            out_ref[0, base + K : base + 2 * K, :] = jnp.where(
                row_at <= col_at, both[:, :K], right
            )
            out_ref[0, 5 * K + place : 5 * K + place + 1, :] = jnp.sum(
                jnp.where(row_at == col_at, right, 0.0), axis=0, keepdims=True
            )

        @pl.when(t < 0)
        def _():
            out_ref[0, base : base + 2 * K, :] = jnp.zeros((2 * K, K), jnp.float32)


def late_kernel(
    owner_ref, rank_ref, panel_rank_ref, got_ref, y_ref, v_ref, out_ref, whole, halves
):
    column = pl.program_id(0)

    @pl.when(column == 0)
    def _():
        for pair in range(PEERS // 2):
            rows = got_ref[16 * pair : 16 * pair + 16, :].astype(jnp.float32)
            for side in range(2):
                part = rows[8 * side : 8 * side + 8]
                peer = 2 * pair + side
                for q in range(FULL):
                    at = 8 * (peer * FULL + q)
                    whole[at : at + 8, :] = part[:, q * K : (q + 1) * K]
                halves[8 * peer : 8 * peer + 8, :] = part[:, FULL * K :]

    right = keep(v_ref[...], panel_rank_ref[0])
    low = lax.broadcasted_iota(jnp.int32, (16, K), 1) < HALF

    def panel_tile(t, which):
        body = whole[pl.ds(which * SPLIT * 8 + t, SPLIT, stride=8), :]
        start = which * PEERS * 4 + t
        end = jnp.where(
            low,
            halves[pl.ds(start, 16, stride=16), :],
            halves[pl.ds(start + 8, 16, stride=16), :],
        )
        return jnp.concatenate([body.astype(jnp.bfloat16), end.astype(jnp.bfloat16)], axis=0)

    for place, t in enumerate(owned_tiles(owner_ref, column)):
        base = 2 * place * K

        @pl.when(t >= 0)
        def _():
            y = keep(y_ref[t], rank_ref[t])
            out_ref[0, base : base + K, :] = tile_dot(right, panel_tile(t, 1))
            out_ref[0, base + K : base + 2 * K, :] = tile_dot(y, panel_tile(t, 0))

        @pl.when(t < 0)
        def _():
            out_ref[0, base : base + 2 * K, :] = jnp.zeros((2 * K, K), jnp.float32)


def final_kernel(early_ref, late_ref, lo_ref, lc_ref, ln_ref, ro_ref, rc_ref):
    row_at = lax.broadcasted_iota(jnp.int32, (K, K), 0)
    col_at = lax.broadcasted_iota(jnp.int32, (K, K), 1)
    gram = early_ref[4 * K : 5 * K, :]
    for place in range(2):
        base = 2 * place * K
        core = late_ref[0, base : base + K, :]
        part_right = late_ref[0, base + K : base + 2 * K, :]
        for c in range(1, COLS):
            core = core + late_ref[c, base : base + K, :]
            part_right = part_right + late_ref[c, base + K : base + 2 * K, :]
        part_left = early_ref[base : base + K, :]
        mixed = early_ref[base + K : base + 2 * K, :]
        turned = mixed.T
        diagonal = early_ref[5 * K + place : 5 * K + place + 1, :]
        lo_ref[place] = jnp.where(row_at <= col_at, mixed, turned)
        ro_ref[place] = jnp.where(
            row_at > col_at, mixed, jnp.where(row_at < col_at, turned, diagonal)
        )
        rc_ref[place] = -part_right
        lc_ref[place] = exact_dot(part_left, core)
        ln_ref[place] = exact_dot(core, exact_dot(gram, core), 0)


def smem():
    return pl.BlockSpec(memory_space=pltpu.SMEM)


def fixed(shape):
    return pl.BlockSpec(shape, lambda c: (0,) * len(shape))


def per_device(panel_u, panel_v, panel_rank, trail_x, trail_y, trail_rank, tile_cols, owner):
    xt = jnp.swapaxes(trail_x, 1, 2)
    yt = jnp.swapaxes(trail_y, 1, 2)
    ut = jnp.swapaxes(panel_u, 1, 2)[0]
    vt = jnp.swapaxes(panel_v, 1, 2)[0]
    owners = owner[:, 0]

    with jax.named_scope("slices_out"):
        kept = keep(jnp.stack([ut, vt]), panel_rank[0])
        whole = kept[:, :SPLIT].reshape(PEERS, FULL * K)
        ends = kept[:, SPLIT:].reshape(PEERS // 2, K)
        wanted = jnp.pad(tile_cols.astype(jnp.bfloat16), (0, HALF - TILES))
        wanted = jnp.broadcast_to(wanted, (PEERS // 2, HALF))
        tail = jnp.stack(
            [
                jnp.concatenate([ends[:, :HALF], wanted], axis=1),
                jnp.concatenate([wanted, ends[:, HALF:]], axis=1),
            ],
            axis=1,
        ).reshape(PEERS, K)
        slices = jnp.concatenate([whole, tail], axis=1)
        held = lax.all_to_all(slices.reshape(PEERS, 1, WIDE), "row", 0, 0).reshape(PEERS, WIDE)

    with jax.named_scope("first_products"):
        early, _ = pl.pallas_call(
            early_kernel,
            grid=(COLS,),
            in_specs=[
                smem(),
                smem(),
                smem(),
                fixed((TILES, S, K)),
                fixed((TILES, S, K)),
                fixed((S, K)),
            ],
            out_specs=[
                pl.BlockSpec((1, EARLY, K), lambda c: (c, 0, 0)),
                fixed((K, K)),
            ],
            out_shape=[
                jax.ShapeDtypeStruct((COLS, EARLY, K), jnp.float32),
                jax.ShapeDtypeStruct((K, K), jnp.float32),
            ],
            compiler_params=pltpu.CompilerParams(vmem_limit_bytes=32 * 1024 * 1024),
            name="first_products",
        )(owners, trail_rank, panel_rank, xt, yt, ut)
        early = lax.psum_scatter(early, "col", scatter_dimension=0, tiled=False)

    with jax.named_scope("tiles_asked_for"):
        at = jnp.where(lax.axis_index("row") % 2 == 0, FULL * K + HALF, FULL * K)
        asked = lax.dynamic_slice(held, (0, at), (PEERS, TILES)).astype(jnp.int32)
        chosen = asked.reshape(PEERS * TILES, 1) == lax.broadcasted_iota(
            jnp.int32, (PEERS * TILES, PEERS), 1
        )
        sent = jnp.dot(
            chosen.astype(jnp.bfloat16), held, preferred_element_type=jnp.float32
        ).astype(jnp.bfloat16)
        got = lax.all_to_all(sent.reshape(PEERS, TILES, WIDE), "row", 0, 0)

    with jax.named_scope("second_products"):
        late = pl.pallas_call(
            late_kernel,
            grid=(COLS,),
            in_specs=[
                smem(),
                smem(),
                smem(),
                fixed((PEERS * TILES, WIDE)),
                fixed((TILES, S, K)),
                fixed((S, K)),
            ],
            out_specs=pl.BlockSpec((1, 4 * K, K), lambda c: (c, 0, 0)),
            out_shape=jax.ShapeDtypeStruct((COLS, 4 * K, K), jnp.float32),
            scratch_shapes=[
                pltpu.VMEM((PEERS * FULL * TILES, K), jnp.float32),
                pltpu.VMEM((PEERS * TILES, K), jnp.float32),
            ],
            compiler_params=pltpu.CompilerParams(vmem_limit_bytes=32 * 1024 * 1024),
            name="second_products",
        )(owners, trail_rank, panel_rank, got.reshape(PEERS * TILES, WIDE), yt, vt)
        late = lax.all_to_all(late, "col", 0, 0)

    with jax.named_scope("owned_results"):
        result = jax.ShapeDtypeStruct((2, K, K), jnp.float32)
        return pl.pallas_call(
            final_kernel,
            out_shape=(result,) * 5,
            compiler_params=pltpu.CompilerParams(vmem_limit_bytes=32 * 1024 * 1024),
            name="owned_results",
        )(early, late)


def solution(mesh):
    placed = (
        P("row", None, "col"),
        P("row", None, "col"),
        P("row"),
        P("row", None, "col"),
        P("row", None, "col"),
        P("row"),
        P("row"),
        P("row", None),
    )
    return jax.shard_map(
        per_device,
        mesh=mesh,
        in_specs=placed,
        out_specs=(P(("row", "col"), None, None),) * 5,
        check_vma=False,
    )
```

time: 1020 us -> 170 us (0.17)
  the two profiles are of different devices: /device:TPU:1 before, /device:TPU:9 now
where the time goes in v1:
time: 170 us
  waiting for transfers between devices  108 us (64%)
  starting transfers between devices  27 us (16%)
  between operations  14.9 us (9%)
  Pallas kernels  9.05 us (5%)
  local copies, waits for them, and re-layouts  5.9 us (3%)
  other arithmetic  2.6 us (2%)
  matrix products  1.7 us (1%)
    unnamed x2, waiting for transfers between devices  62.8 us
    all_to_all x1, waiting for transfers between devices, per_device(): got = lax.all_to_all(sent.reshape(PEERS, TILES, WIDE), 'row', 0, 0)  31.9 us
    all_to_all x1, starting transfers between devices, per_device(): lax.all_to_all(slices.reshape(PEERS, 1, WIDE), 'row', 0, 0)  16.9 us
    all_to_all x1, waiting for transfers between devices, per_device(): lax.all_to_all(slices.reshape(PEERS, 1, WIDE), 'row', 0, 0)  13.8 us
    all_to_all x1, starting transfers between devices, per_device(): got = lax.all_to_all(sent.reshape(PEERS, TILES, WIDE), 'row', 0, 0)  5.15 us
    unnamed x20, local copies, waits for them, and re-layouts  4.97 us
    all_to_all x1, starting transfers between devices, per_device(): late = lax.all_to_all(late, 'col', 0, 0)  4.88 us
    pallas_call x1, Pallas kernels, per_device(): pl.pallas_call(early_kernel, grid=(COLS,), in_specs=[smem(), smem(), smem...  4.19 us
  transfers between devices with their start and end apart: 4, of which 3 were waited for; matrix products, arithmetic and copies ran while one was open for 0% of the time, Pallas kernels for 4%

profile of v1, /device:TPU:9, one launch (start us, length us, event | category | flops | bytes accessed | tf_op | source)
XLA Modules:
  0.0 169.6 jit_solution(540775518164809952)
XLA Ops:
  7.8 1.0 maximum_select_fusion
  8.8 0.7 convert_element_type.19
  9.5 0.1 fusion.4
  9.6 0.1 maximum_bitcast_fusion.1
  9.7 0.2 reshape.40
  9.9 0.5 broadcast.8
  10.4 0.7 reduce.4
  11.1 0.9 reshape.56
  12.0 16.9 %all-to-all-start = ((bf16[64,2,704]{2,1,0:T(2,128)(2,1)}), bf16[64,2,704]{2,1,0:T(2,128)(2,1)S(1)}, u32[]{:S(2)}, u32[]{:S(2)}) async-start(bf16[64,2,704]{2,1,0:T(2,128)(2,1)} %reshape.56), calls=%async_computation | async-start | bytes 393216 | tf_op jit(solution)/shard_map/slices_out/all_to_all | solution.py:182
  28.9 13.8 %all-to-all-done = bf16[64,2,704]{2,1,0:T(2,128)(2,1)S(1)} async-done(((bf16[64,2,704]{2,1,0:T(2,128)(2,1)}), bf16[64,2,704]{2,1,0:T(2,128)(2,1)S(1)}, u32[]{:S(2)}, u32[]{:S(2)}) %all-to-all-start) | async-done | bytes 180256 | tf_op jit(solution)/shard_map/slices_out/all_to_all | solution.py:182
  42.7 0.2 reshape.57
  42.9 0.2 convert_reduce_fusion
  43.1 0.1 reshape.47
  43.2 0.0 copy-start.1
  43.2 0.0 copy-start.3
  43.2 0.0 copy-start.4
  43.3 0.0 copy-start.7
  43.3 0.0 copy-start.8
  43.3 1.7 %fusion = bf16[64,8,1408]{2,1,0:T(8,128)(2,1)} fusion(bf16[64,1,1408]{2,1,0:T(2,128)(2,1)S(1)} %reshape.57, s32[512]{0:T(512)S(1)} %reshape.47), kind=kOutput, calls=%fused_computation.1 | convolution fusion | flops 93028352 | bytes 1624064 | tf_op jit(solution)/shard_map/tiles_asked_for/dot_general | solution.py:215
  45.0 5.1 %all-to-all-start.1 = ((bf16[64,8,1408]{2,1,0:T(8,128)(2,1)}), bf16[64,8,1408]{2,1,0:T(8,128)(2,1)S(1)}, u32[]{:S(2)}, u32[]{:S(2)}) async-start(bf16[64,8,1408]{2,1,0:T(8,128)(2,1)} %fusion), calls=%async_computation.1 | async-start | bytes 2883584 | tf_op jit(solution)/shard_map/tiles_asked_for/all_to_all | solution.py:218
  50.1 0.0 copy-start.5
  50.1 0.0 reduce-scatter.5.cloned.1.call-start
  50.2 4.2 %first_products.1 = (f32[8,648,128]{2,1,0:T(8,128)S(1)}, f32[128,128]{1,0:T(8,128)}) custom-call(s32[8]{0:T(128)S(1)} %bitcast.36, s32[8]{0:T(128)S(1)} %copy-done.8, s32[1]{0:T(128)} %copy.24.panel_rank_ref, bf16[8,336,128]{2,1,0:T(8,128)(2,1)S(1)} %bitcast.30, bf16[8,336,128]{2,1,0:T(8,128)(2,1)S(1)} %bitcast.28, bf16[336,128]{1,0:T(8,128)(2,1)S(1)} %bitcast.32), custom_call_target="tpu_custom_call" | custom-call | tf_op jit(solution)/shard_map/first_products/first_products/pallas_call | solution.py:185
  54.4 1.5 copy-done.2
  56.0 0.0 reduce-scatter.5.cloned.1.call-update
  56.0 31.9 %all-to-all-done.1 = bf16[64,8,1408]{2,1,0:T(8,128)(2,1)S(1)} async-done(((bf16[64,8,1408]{2,1,0:T(8,128)(2,1)}), bf16[64,8,1408]{2,1,0:T(8,128)(2,1)S(1)}, u32[]{:S(2)}, u32[]{:S(2)}) %all-to-all-start.1) | async-done | bytes 1441824 | tf_op jit(solution)/shard_map/tiles_asked_for/all_to_all | solution.py:218
  87.8 3.4 %second_products.1 = f32[8,512,128]{2,1,0:T(8,128)S(1)} custom-call(s32[8]{0:T(128)S(1)} %bitcast.37, s32[8]{0:T(128)S(1)} %copy-done.8, s32[1]{0:T(128)} %copy.24.panel_rank_ref, bf16[512,1408]{1,0:T(8,128)(2,1)S(1)} %bitcast.27, bf16[8,336,128]{2,1,0:T(8,128)(2,1)S(1)} %bitcast.29, bf16[336,128]{1,0:T(8,128)(2,1)S(1)} %bitcast.34), custom_call_target="tpu_custom_call" | custom-call | tf_op jit(solution)/shard_map/second_products/second_products/pallas_call | solution.py:221
  91.2 1.3 copy-done
  92.5 4.9 %all-to-all-start.2 = ((f32[8,512,128]{2,1,0:T(8,128)}), f32[8,512,128]{2,1,0:T(8,128)S(1)}, u32[]{:S(2)}, u32[]{:S(2)}) async-start(f32[8,512,128]{2,1,0:T(8,128)} %copy-done), calls=%async_computation.2 | async-start | bytes 4194304 | tf_op jit(solution)/shard_map/second_products/all_to_all | solution.py:241
  97.4 62.8 %reduce-scatter.5.cloned.1.call-done = f32[1,648,128]{2,1,0:T(8,128)} async-done(((f32[8,648,128]{2,1,0:T(8,128)}), f32[1,648,128]{2,1,0:T(8,128)}) %reduce-scatter.5.cloned.1.call-update) | async-done | bytes 331792
  160.2 1.0 copy-done.6
  161.2 1.5 owned_results.1
  (18 shorter events, 0.1 us)
Async XLA Ops:
  12.0 30.7 %all-to-all-start = ((bf16[64,2,704]{2,1,0:T(2,128)(2,1)}), bf16[64,2,704]{2,1,0:T(2,128)(2,1)S(1)}, u32[]{:S(2)}, u32[]{:S(2)}) async-start(bf16[64,2,704]{2,1,0:T(2,128)(2,1)} %reshape.56), calls=%async_computation | async-start | bytes 393216 | tf_op jit(solution)/shard_map/slices_out/all_to_all | solution.py:182
  43.2 7.0 %copy-start.1 = (bf16[8,128,336]{1,2,0:T(8,128)(2,1)S(1)}, bf16[8,128,336]{1,2,0:T(8,128)(2,1)}, u32[]{:S(2)}) copy-start(bf16[8,128,336]{1,2,0:T(8,128)(2,1)} %param.12) | copy-start | bytes 2064388
  43.2 7.0 %copy-start.3 = (bf16[8,128,336]{1,2,0:T(8,128)(2,1)S(1)}, bf16[8,128,336]{1,2,0:T(8,128)(2,1)}, u32[]{:S(2)}) copy-start(bf16[8,128,336]{1,2,0:T(8,128)(2,1)} %param.11) | copy-start | bytes 2064388
  43.2 7.0 %copy-start.4 = (bf16[1,128,336]{1,2,0:T(8,128)(2,1)S(1)}, bf16[1,128,336]{1,2,0:T(8,128)(2,1)}, u32[]{:S(2)}) copy-start(bf16[1,128,336]{1,2,0:T(8,128)(2,1)} %param.8) | copy-start | bytes 258052
  43.3 7.0 %copy-start.7 = (s32[8,1]{0,1:T(1,128)S(1)}, s32[8,1]{0,1:T(1,128)}, u32[]{:S(2)}) copy-start(s32[8,1]{0,1:T(1,128)} %param.15) | copy-start | bytes 100
  43.3 7.0 %copy-start.8 = (s32[8]{0:T(128)S(1)}, s32[8]{0:T(128)}, u32[]{:S(2)}) copy-start(s32[8]{0:T(128)} %rank_ref.3) | copy-start | bytes 100
  45.0 42.9 %all-to-all-start.1 = ((bf16[64,8,1408]{2,1,0:T(8,128)(2,1)}), bf16[64,8,1408]{2,1,0:T(8,128)(2,1)S(1)}, u32[]{:S(2)}, u32[]{:S(2)}) async-start(bf16[64,8,1408]{2,1,0:T(8,128)(2,1)} %fusion), calls=%async_computation.1 | async-start | bytes 2883584 | tf_op jit(solution)/shard_map/tiles_asked_for/all_to_all | solution.py:218
  50.1 37.7 %copy-start.5 = (bf16[1,128,336]{1,2,0:T(8,128)(2,1)S(1)}, bf16[1,128,336]{1,2,0:T(8,128)(2,1)}, u32[]{:S(2)}) copy-start(bf16[1,128,336]{1,2,0:T(8,128)(2,1)} %param.9) | copy-start | bytes 258052
  50.1 110.1 %reduce-scatter.5.cloned.1.call-start = ((), (), s32[]{:S(2)}) async-start(), calls=%async_computation.4 | async-start | bytes 2985984
  54.4 1.5 copy-start.2
  91.2 1.3 copy-start
  92.5 67.7 %all-to-all-start.2 = ((f32[8,512,128]{2,1,0:T(8,128)}), f32[8,512,128]{2,1,0:T(8,128)S(1)}, u32[]{:S(2)}, u32[]{:S(2)}) async-start(f32[8,512,128]{2,1,0:T(8,128)} %copy-done), calls=%async_computation.2 | async-start | bytes 4194304 | tf_op jit(solution)/shard_map/second_products/all_to_all | solution.py:241
  160.2 1.0 copy-start.6
Sparse Core Ops, SparseCore 0:
  56.1 104.0 reduce-scatter.4

commit v2 on v1

v2 whole, which is shorter than its diff:
```python
import jax
import jax.numpy as jnp
from jax import lax
from jax.experimental import pallas as pl
from jax.experimental.pallas import tpu as pltpu
from jax.sharding import PartitionSpec as P

K = 128
S = 336
TILES = 8
PEERS = 64
COLS = 8
EACH = 10
SLICED = EACH * PEERS // 2
SHARED = S - SLICED
WIDE = (EACH + 1) * K
BLOCK = 16
HALF = K // 2
LONG = 3 * K
PART = K // COLS
EARLY = TILES * PART
FIRST = EARLY + 8
SECOND = EARLY + PART
OWNED = 8 * PART + PART + 8
EARLY_AT = [
    slice(at, at + 2 * PART)
    for base in (0, FIRST)
    for at in range(base, base + EARLY, 2 * PART)
]
VMEM = 32 * 1024 * 1024


def tile_dot(first, second):
    return lax.dot_general(
        first, second, (((0,), (0,)), ((), ())), preferred_element_type=jnp.float32
    )


def plain_dot(first, second):
    return jnp.dot(first, second, preferred_element_type=jnp.float32)


def exact_dot(first, second, lhs_dim=1):
    return lax.dot_general(
        first,
        second,
        (((lhs_dim,), (0,)), ((), ())),
        precision=lax.Precision.HIGHEST,
        preferred_element_type=jnp.float32,
    )


def keep(block, rank):
    lane = lax.broadcasted_iota(jnp.int32, block.shape, block.ndim - 1)
    return jnp.where(lane < rank, block, jnp.zeros_like(block))


def owned_tiles(owner_ref, column):
    first = jnp.int32(-1)
    second = jnp.int32(-1)
    for t in range(TILES):
        mine = owner_ref[t] == column
        second = jnp.where(mine & (first >= 0), t, second)
        first = jnp.where(mine & (first < 0), t, first)
    return first, second


def slices_kernel(cols_ref, kept_ref, slices_ref, rows, blocks):
    lane = lax.broadcasted_iota(jnp.int32, (SHARED, K), 1)
    wanted = jnp.zeros((SHARED, K), jnp.int32)
    for t in range(TILES):
        wanted = jnp.where(lane % HALF == t, cols_ref[t], wanted)
    wanted = wanted.astype(jnp.float32)
    blocks[...] = jnp.zeros_like(blocks)
    for which in range(2):
        kept = kept_ref[which]
        rows[which * SLICED : (which + 1) * SLICED, :] = kept[:SLICED].astype(jnp.float32)
        ends = kept[SLICED:].astype(jnp.float32)
        at = which * PEERS // 2 * BLOCK + EACH
        blocks[pl.ds(at, SHARED, stride=2 * BLOCK), :] = jnp.where(lane < HALF, ends, wanted)
        blocks[pl.ds(at + BLOCK, SHARED, stride=2 * BLOCK), :] = jnp.where(
            lane < HALF, wanted, ends
        )
    for q in range(EACH):
        blocks[pl.ds(q, PEERS, stride=BLOCK), :] = rows[pl.ds(q, PEERS, stride=EACH), :]
    slices_ref[...] = blocks[...].astype(jnp.bfloat16)


def turned(block):
    filler = jnp.zeros((LONG - S, K), block.dtype)
    return jnp.concatenate([block, filler], axis=0).T


def early_kernel(
    rank_ref,
    kept_ref,
    x_ref,
    y_ref,
    first_sent,
    first_kept,
    second_sent,
    second_kept,
    right_turned,
    y_turned,
    products,
    diagonals,
    gram,
):
    left = kept_ref[0]
    right_turned[...] = turned(kept_ref[1])
    gram[...] = tile_dot(left, left)
    row_at = lax.broadcasted_iota(jnp.int32, (K, K), 0)
    col_at = lax.broadcasted_iota(jnp.int32, (K, K), 1)
    for t in range(TILES):
        x = keep(x_ref[t], rank_ref[t])
        y = keep(y_ref[t], rank_ref[t])
        y_turned[t] = turned(y)
        both = tile_dot(x, jnp.concatenate([x, left], axis=1))
        right = tile_dot(y, y)
        products[t, 0] = both[:, K:]
        products[t, 1] = jnp.where(row_at <= col_at, both[:, :K], right)
        diagonal = jnp.sum(jnp.where(row_at == col_at, right, 0.0), axis=0, keepdims=True)
        diagonals[t] = jnp.broadcast_to(diagonal, (8, K))

    here = lax.axis_index("col")
    firsts = [(first_kept, 0), (first_sent, 0), (first_sent, 1), (first_kept, 1)]
    seconds = [(second_kept, 0), (second_kept, 1), (second_sent, 1), (second_sent, 0)]
    for away in range(COLS):
        column = here ^ away
        start = pl.multiple_of(column * PART, PART)
        along, across = away // 2, away % 2
        for low, (ref, at) in ((0, firsts[along]), (TILES // 2, seconds[along])):
            for n in range(TILES):
                ref[at, across, n * PART : (n + 1) * PART, :] = products[
                    low + n // 2, n % 2, pl.ds(start, PART), :
                ]
        ref, at = firsts[along]
        ref[at, across, EARLY:, :] = diagonals[column]
        ref, at = seconds[along]
        ref[at, across, EARLY:, :] = gram[pl.ds(start, PART), :]


def late_kernel(
    got_ref, right_ref, y_ref, out_ref, rows, halves
):
    for pair in range(PEERS // 2):
        part = got_ref[16 * pair : 16 * pair + 16, :].astype(jnp.float32)
        for side in range(2):
            peer = 2 * pair + side
            mine = part[8 * side : 8 * side + 8]
            for q in range(EACH):
                at = 8 * (peer * EACH + q)
                rows[at : at + 8, :] = mine[:, q * K : (q + 1) * K]
            halves[8 * peer : 8 * peer + 8, :] = mine[:, EACH * K :]
    right = right_ref[...]
    filler = jnp.zeros((LONG - S, K), jnp.bfloat16)
    low = lax.broadcasted_iota(jnp.int32, (SHARED, K), 1) < HALF

    def panel_tile(t, which):
        body = rows[pl.ds(which * SLICED * 8 + t, SLICED, stride=8), :]
        at = which * PEERS * 4 + t
        end = jnp.where(
            low,
            halves[pl.ds(at, SHARED, stride=16), :],
            halves[pl.ds(at + 8, SHARED, stride=16), :],
        )
        return jnp.concatenate(
            [body.astype(jnp.bfloat16), end.astype(jnp.bfloat16), filler], axis=0
        )

    for t in range(TILES):
        core = plain_dot(right, panel_tile(t, 1))
        part_right = plain_dot(y_ref[t], panel_tile(t, 0))
        for c in range(COLS):
            base = 2 * t * PART
            out_ref[c, base : base + PART, :] = core[c * PART : (c + 1) * PART]
            out_ref[c, base + PART : base + 2 * PART, :] = part_right[c * PART : (c + 1) * PART]


def route_kernel(owner_ref, kept_ref, came_ref, late_ref, out_ref, sums):
    for t in range(TILES):
        base = 2 * t * PART
        sums[t, : 2 * PART, :] = kept_ref[EARLY_AT[t], :] + came_ref[EARLY_AT[t], :]
        total = late_ref[0, base : base + 2 * PART, :]
        for c in range(1, COLS):
            total = total + late_ref[c, base : base + 2 * PART, :]
        sums[t, 2 * PART :, :] = total
    diagonal = kept_ref[EARLY:FIRST, :] + came_ref[EARLY:FIRST, :]
    gram = kept_ref[FIRST + EARLY :, :] + came_ref[FIRST + EARLY :, :]
    for column in range(COLS):
        for place, t in enumerate(owned_tiles(owner_ref, column)):
            there = slice(4 * place * PART, 4 * (place + 1) * PART)

            @pl.when(t >= 0)
            def _():
                out_ref[column, there, :] = sums[t]

            @pl.when(t < 0)
            def _():
                out_ref[column, there, :] = jnp.zeros((4 * PART, K), jnp.float32)

        out_ref[column, 8 * PART : 9 * PART, :] = gram
        out_ref[column, 9 * PART :, :] = diagonal


def final_kernel(owner_ref, got_ref, lo_ref, lc_ref, ln_ref, ro_ref, rc_ref):
    row_at = lax.broadcasted_iota(jnp.int32, (K, K), 0)
    col_at = lax.broadcasted_iota(jnp.int32, (K, K), 1)

    def whole(at):
        return jnp.concatenate(
            [got_ref[c, at * PART : (at + 1) * PART, :] for c in range(COLS)], axis=0
        )

    gram = whole(8)
    for place, t in enumerate(owned_tiles(owner_ref, lax.axis_index("col"))):
        part_left = whole(4 * place)
        mixed = whole(4 * place + 1)
        core = whole(4 * place + 2)
        part_right = whole(4 * place + 3)
        diagonal = jnp.where(t >= 0, got_ref[jnp.maximum(t, 0), 9 * PART :, :][:1], 0.0)
        across = mixed.T
        lo_ref[place] = jnp.where(row_at <= col_at, mixed, across)
        ro_ref[place] = jnp.where(
            row_at > col_at, mixed, jnp.where(row_at < col_at, across, diagonal)
        )
        rc_ref[place] = -part_right
        lc_ref[place] = exact_dot(part_left, core)
        ln_ref[place] = exact_dot(core, exact_dot(gram, core), 0)


def swapped(block, away):
    return lax.ppermute(block, "col", [(c, c ^ away) for c in range(COLS)])


def cost(micros):
    return pl.CostEstimate(flops=micros * 1000000000, bytes_accessed=0, transcendentals=0)


def smem(count):
    return [pl.BlockSpec(memory_space=pltpu.SMEM)] * count


def vmem(count):
    return [pl.BlockSpec(memory_space=pltpu.VMEM)] * count


def per_device(panel_u, panel_v, panel_rank, trail_x, trail_y, trail_rank, tile_cols, owner):
    params = pltpu.CompilerParams(vmem_limit_bytes=VMEM)
    xt = jnp.swapaxes(trail_x, 1, 2)
    yt = jnp.swapaxes(trail_y, 1, 2)
    ut = jnp.swapaxes(panel_u, 1, 2)[0]
    vt = jnp.swapaxes(panel_v, 1, 2)[0]
    owners = owner[:, 0]

    with jax.named_scope("slices_out"):
        kept = keep(jnp.stack([ut, vt]), panel_rank[0])
        slices = pl.pallas_call(
            slices_kernel,
            in_specs=smem(1) + vmem(1),
            out_shape=jax.ShapeDtypeStruct((PEERS * BLOCK, K), jnp.bfloat16),
            scratch_shapes=[
                pltpu.VMEM((2 * SLICED, K), jnp.float32),
                pltpu.VMEM((PEERS * BLOCK, K), jnp.float32),
            ],
            compiler_params=params,
            cost_estimate=cost(1),
            name="slices_out",
        )(tile_cols, kept)
        held = lax.all_to_all(slices.reshape(PEERS, BLOCK, K), "row", 0, 0)
        held = held.reshape(PEERS, BLOCK * K)

    with jax.named_scope("first_products"):
        first = jax.ShapeDtypeStruct((2, 2, FIRST, K), jnp.float32)
        second = jax.ShapeDtypeStruct((2, 2, SECOND, K), jnp.float32)
        *pieces, right_turned, y_turned = pl.pallas_call(
            early_kernel,
            in_specs=smem(1) + vmem(3),
            out_shape=[
                first,
                first,
                second,
                second,
                jax.ShapeDtypeStruct((K, LONG), jnp.bfloat16),
                jax.ShapeDtypeStruct((TILES, K, LONG), jnp.bfloat16),
            ],
            scratch_shapes=[
                pltpu.VMEM((TILES, 2, K, K), jnp.float32),
                pltpu.VMEM((TILES, 8, K), jnp.float32),
                pltpu.VMEM((K, K), jnp.float32),
            ],
            compiler_params=params,
            cost_estimate=cost(4),
            name="first_products",
        )(trail_rank, kept, xt, yt)
        held, *_ = lax.optimization_barrier((held, *pieces))

    with jax.named_scope("first_sum"):
        first_sent, first_kept, second_sent, second_kept = pieces
        first = first_kept + swapped(first_sent, 2)
        second = second_kept + swapped(second_sent, 6)
        first = first[0] + swapped(first[1], 6)
        second = second[0] + swapped(second[1], 2)
        early_kept = jnp.concatenate([first[0], second[0]])
        early_came = swapped(jnp.concatenate([first[1], second[1]]), 1)

    with jax.named_scope("tiles_asked_for"):
        at = jnp.where(lax.axis_index("row") % 2 == 0, EACH * K + HALF, EACH * K)
        asked = lax.dynamic_slice(held, (0, at), (PEERS, TILES)).astype(jnp.int32)
        chosen = asked.reshape(PEERS * TILES, 1) == lax.broadcasted_iota(
            jnp.int32, (PEERS * TILES, PEERS), 1
        )
        sent = jnp.dot(
            chosen.astype(jnp.bfloat16), held[:, :WIDE], preferred_element_type=jnp.float32
        ).astype(jnp.bfloat16)
        got = lax.all_to_all(sent.reshape(PEERS, TILES, WIDE), "row", 0, 0)
        got, early_came = lax.optimization_barrier((got, early_came))

    with jax.named_scope("second_products"):
        late = pl.pallas_call(
            late_kernel,
            in_specs=vmem(3),
            out_shape=jax.ShapeDtypeStruct((COLS, 2 * K, K), jnp.float32),
            scratch_shapes=[
                pltpu.VMEM((PEERS * EACH * TILES, K), jnp.float32),
                pltpu.VMEM((PEERS * TILES, K), jnp.float32),
            ],
            compiler_params=params,
            cost_estimate=cost(4),
            name="second_products",
        )(got.reshape(PEERS * TILES, WIDE), right_turned, y_turned)
        late = lax.all_to_all(late, "col", 0, 0)

    with jax.named_scope("parts_to_owners"):
        owned = pl.pallas_call(
            route_kernel,
            in_specs=smem(1) + vmem(3),
            out_shape=jax.ShapeDtypeStruct((COLS, OWNED, K), jnp.float32),
            scratch_shapes=[pltpu.VMEM((TILES, 4 * PART, K), jnp.float32)],
            compiler_params=params,
            cost_estimate=cost(1),
            name="parts_to_owners",
        )(owners, early_kept, early_came, late)
        owned = lax.all_to_all(owned, "col", 0, 0)

    with jax.named_scope("owned_results"):
        result = jax.ShapeDtypeStruct((2, K, K), jnp.float32)
        return pl.pallas_call(
            final_kernel,
            in_specs=smem(1) + vmem(1),
            out_shape=(result,) * 5,
            compiler_params=params,
            name="owned_results",
        )(owners, owned)


def solution(mesh):
    placed = (
        P("row", None, "col"),
        P("row", None, "col"),
        P("row"),
        P("row", None, "col"),
        P("row", None, "col"),
        P("row"),
        P("row"),
        P("row", None),
    )
    return jax.shard_map(
        per_device,
        mesh=mesh,
        in_specs=placed,
        out_specs=(P(("row", "col"), None, None),) * 5,
        check_vma=False,
    )
```

time: 170 us -> 122 us (0.72)
  the two profiles are of different devices: /device:TPU:9 before, /device:TPU:24 now
where the time goes in v2:
time: 122 us
  waiting for transfers between devices  49 us (40%)
  starting transfers between devices  44.6 us (37%)
  blocking collectives  14 us (11%)
  Pallas kernels  7.88 us (6%)
  local copies, waits for them, and re-layouts  1.75 us (1%)
  matrix products  1.71 us (1%)
  between operations  1.49 us (1%)
    ppermute x5, waiting for transfers between devices, swapped(): return lax.ppermute(block, 'col', [(c, c ^ away) for c in range(COLS)])  20.5 us
    ppermute x5, starting transfers between devices, swapped(): return lax.ppermute(block, 'col', [(c, c ^ away) for c in range(COLS)])  17.7 us
    all_to_all x1, starting transfers between devices, per_device(): held = lax.all_to_all(slices.reshape(PEERS, BLOCK, K), 'row', 0, 0)  16.4 us
    all_to_all x1, waiting for transfers between devices, per_device(): late = lax.all_to_all(late, 'col', 0, 0)  15.6 us
    all_to_all x1, blocking collectives, per_device(): owned = lax.all_to_all(owned, 'col', 0, 0)  14 us
    all_to_all x1, waiting for transfers between devices, per_device(): held = lax.all_to_all(slices.reshape(PEERS, BLOCK, K), 'row', 0, 0)  11.7 us
    all_to_all x1, starting transfers between devices, per_device(): got = lax.all_to_all(sent.reshape(PEERS, TILES, WIDE), 'row', 0, 0)  6.04 us
    all_to_all x1, starting transfers between devices, per_device(): late = lax.all_to_all(late, 'col', 0, 0)  4.43 us
  transfers between devices with their start and end apart: 8, of which 7 were waited for; matrix products, arithmetic and copies ran while one was open for 0% of the time, Pallas kernels for 1%

profile of v2, /device:TPU:24, one launch (start us, length us, event | category | flops | bytes accessed | tf_op | source)
XLA Modules:
  0.0 121.6 jit_solution(7819154162624244247)
XLA Ops:
  1.3 1.0 maximum_select_fusion.kept_ref
  2.2 0.0 copy-start.3
  2.3 0.6 copy-done.3
  2.9 1.4 %slices_out.1 = bf16[1024,128]{1,0:T(8,128)(2,1)} custom-call(s32[8]{0:T(128)S(1)} %copy-done.3, bf16[2,336,128]{2,1,0:T(8,128)(2,1)S(1)} %maximum_select_fusion.kept_ref), custom_call_target="tpu_custom_call" | custom-call | flops 1000000000 | tf_op jit(solution)/shard_map/slices_out/slices_out/pallas_call | solution.py:258
  4.4 16.4 %all-to-all-start = ((bf16[64,16,128]{2,1,0:T(8,128)(2,1)}), bf16[64,16,128]{2,1,0:T(8,128)(2,1)S(1)}, u32[]{:S(2)}, u32[]{:S(2)}) async-start(bf16[64,16,128]{2,1,0:T(8,128)(2,1)} %bitcast.12), calls=%async_computation | async-start | bytes 524288 | tf_op jit(solution)/shard_map/slices_out/all_to_all | solution.py:270
  20.8 0.0 copy-done.1
  20.8 0.0 copy-done.2
  20.8 1.4 %first_products.1 = (f32[2,2,136,128]{3,2,1,0:T(8,128)S(1)}, f32[2,2,136,128]{3,2,1,0:T(8,128)S(1)}, f32[2,2,144,128]{3,2,1,0:T(8,128)S(1)}, f32[2,2,144,128]{3,...) custom-call(s32[8]{0:T(128)S(1)} %copy-done.4, ...), custom_call_target="tpu_custom_call" | custom-call | flops 4000000000 | tf_op jit(solution)/shard_map/first_products/first_products/pallas_call | solution.py:276
  22.2 0.9 copy-done.5
  23.1 11.7 %all-to-all-done = bf16[64,16,128]{2,1,0:T(8,128)(2,1)S(1)} async-done(((bf16[64,16,128]{2,1,0:T(8,128)(2,1)}), bf16[64,16,128]{2,1,0:T(8,128)(2,1)S(1)}, u32[]{:S(2)}, u32[]{:S(2)}) %all-to-all-start) | async-done | bytes 262176 | tf_op jit(solution)/shard_map/slices_out/all_to_all | solution.py:270
  34.8 0.1 copy.15
  34.8 0.1 dynamic-slice_convert_fusion
  34.9 0.1 reshape.28
  35.0 1.7 %fusion = bf16[64,8,1408]{2,1,0:T(8,128)(2,1)} fusion(bf16[64,2048]{1,0:T(8,128)(2,1)S(1)} %bitcast.42, s32[512]{0:T(512)S(1)} %reshape.28), kind=kOutput, calls=%fused_computation.1 | convolution fusion | flops 93028352 | bytes 1624064 | tf_op jit(solution)/shard_map/tiles_asked_for/dot_general | solution.py:313
  36.7 6.0 %all-to-all-start.1 = ((bf16[64,8,1408]{2,1,0:T(8,128)(2,1)}), bf16[64,8,1408]{2,1,0:T(8,128)(2,1)S(1)}, u32[]{:S(2)}, u32[]{:S(2)}) async-start(bf16[64,8,1408]{2,1,0:T(8,128)(2,1)} %fusion), calls=%async_computation.1 | async-start | bytes 2883584 | tf_op jit(solution)/shard_map/tiles_asked_for/all_to_all | solution.py:316
  42.8 3.4 %collective-permute-start = (f32[2,2,136,128]{3,2,1,0:T(8,128)S(1)}, f32[2,2,136,128]{3,2,1,0:T(8,128)S(1)}, u32[]{:S(2)}, u32[]{:S(2)}) collective-permute-start(f32[2,2,136,128]{3,2,1,0:T(8,128)S(1)} %get-tuple-element.15), channel_id=1, source_target_pairs={{0,2},{1,3},{2,0},{3,1},{4,6},{5,7},{6,4},{7,5},{8,10},{9,11},{10,... | collective-permute-start | bytes 835592 | tf_op jit(solution)/shard_map/first_sum/ppermute | solution.py:233
  46.2 4.0 %collective-permute-start.2 = (f32[2,2,144,128]{3,2,1,0:T(8,128)S(1)}, f32[2,2,144,128]{3,2,1,0:T(8,128)S(1)}, u32[]{:S(2)}, u32[]{:S(2)}) collective-permute-start(f32[2,2,144,128]{3,2,1,0:T(8,128)S(1)} %get-tuple-element.17), channel_id=1, source_target_pairs={{0,6},{1,7},{2,4},{3,5},{4,2},{5,3},{6,0},{7,1},{8,14},{9,15},{10,... | collective-permute-start | bytes 884744 | tf_op jit(solution)/shard_map/first_sum/ppermute | solution.py:233
  50.2 3.2 %collective-permute-done = f32[2,2,136,128]{3,2,1,0:T(8,128)S(1)} collective-permute-done((f32[2,2,136,128]{3,2,1,0:T(8,128)S(1)}, f32[2,2,136,128]{3,2,1,0:T(8,128)S(1)}, u32[]{:S(2)}, u32[]{:S(2)}) %collective-permute-start) | collective-permute-done | bytes 278560 | tf_op jit(solution)/shard_map/first_sum/ppermute | solution.py:233
  53.4 4.8 %collective-permute-start.1 = (f32[2,136,128]{2,1,0:T(8,128)S(1)}, f32[2,136,128]{2,1,0:T(8,128)S(1)}, u32[]{:S(2)}, u32[]{:S(2)}) collective-permute-start(f32[2,136,128]{2,1,0:T(8,128)S(1)} %slice_bitcast_fusion.2), channel_id=1, source_target_pairs={{0,6},{1,7},{2,4},{3,5},{4,2},{5,3},{6,0},{7,1},{8,14},{9,15},{10,... | collective-permute-start | bytes 417800 | tf_op jit(solution)/shard_map/first_sum/ppermute | solution.py:233
  58.2 0.0 collective-permute-done.2
  58.3 2.1 %collective-permute-start.3 = (f32[2,144,128]{2,1,0:T(8,128)S(1)}, f32[2,144,128]{2,1,0:T(8,128)S(1)}, u32[]{:S(2)}, u32[]{:S(2)}) collective-permute-start(f32[2,144,128]{2,1,0:T(8,128)S(1)} %slice_bitcast_fusion), channel_id=1, source_target_pairs={{0,2},{1,3},{2,0},{3,1},{4,6},{5,7},{6,4},{7,5},{8,10},{9,11},{10,... | collective-permute-start | bytes 442376 | tf_op jit(solution)/shard_map/first_sum/ppermute | solution.py:233
  60.5 1.3 %collective-permute-done.1 = f32[2,136,128]{2,1,0:T(8,128)S(1)} collective-permute-done((f32[2,136,128]{2,1,0:T(8,128)S(1)}, f32[2,136,128]{2,1,0:T(8,128)S(1)}, u32[]{:S(2)}, u32[]{:S(2)}) %collective-permute-start.1) | collective-permute-done | bytes 139296 | tf_op jit(solution)/shard_map/first_sum/ppermute | solution.py:233
  61.8 3.6 %collective-permute-done.3 = f32[2,144,128]{2,1,0:T(8,128)S(1)} collective-permute-done((f32[2,144,128]{2,1,0:T(8,128)S(1)}, f32[2,144,128]{2,1,0:T(8,128)S(1)}, u32[]{:S(2)}, u32[]{:S(2)}) %collective-permute-start.3) | collective-permute-done | bytes 147488 | tf_op jit(solution)/shard_map/first_sum/ppermute | solution.py:233
  65.4 3.4 %collective-permute-start.4 = (f32[280,128]{1,0:T(8,128)S(1)}, f32[280,128]{1,0:T(8,128)S(1)}, u32[]{:S(2)}, u32[]{:S(2)}) collective-permute-start(f32[280,128]{1,0:T(8,128)S(1)} %pad_maximum_fusion.1), channel_id=1, source_target_pairs={{0,1},{1,0},{2,3},{3,2},{4,5},{5,4},{6,7},{7,6},{8,9},{9,8},{10,11... | collective-permute-start | bytes 430088 | tf_op jit(solution)/shard_map/first_sum/ppermute | solution.py:233
  68.8 12.4 %collective-permute-done.4.came_ref = f32[280,128]{1,0:T(8,128)S(1)} collective-permute-done((f32[280,128]{1,0:T(8,128)S(1)}, f32[280,128]{1,0:T(8,128)S(1)}, u32[]{:S(2)}, u32[]{:S(2)}) %collective-permute-start.4) | collective-permute-done | bytes 143392 | tf_op jit(solution)/shard_map/first_sum/ppermute | solution.py:233
  81.3 1.2 %all-to-all-done.1 = bf16[64,8,1408]{2,1,0:T(8,128)(2,1)S(1)} async-done(((bf16[64,8,1408]{2,1,0:T(8,128)(2,1)}), bf16[64,8,1408]{2,1,0:T(8,128)(2,1)S(1)}, u32[]{:S(2)}, u32[]{:S(2)}) %all-to-all-start.1) | async-done | bytes 1441824 | tf_op jit(solution)/shard_map/tiles_asked_for/all_to_all | solution.py:316
  82.5 2.1 %second_products.1 = f32[8,256,128]{2,1,0:T(8,128)} custom-call(bf16[512,1408]{1,0:T(8,128)(2,1)S(1)} %bitcast.35, bf16[128,384]{1,0:T(8,128)(2,1)S(1)} %get-tuple-element.21.right_ref, bf16[8,128,384]{2,1,0:T(8,128)(2,1)S(1)} %copy-done.6), custom_call_target="tpu_custom_call" | custom-call | flops 4000000000 | tf_op jit(solution)/shard_map/second_products/second_products/pallas_call | solution.py:320
  84.6 4.4 %all-to-all-start.2 = ((f32[8,256,128]{2,1,0:T(8,128)}), f32[8,256,128]{2,1,0:T(8,128)S(1)}, u32[]{:S(2)}, u32[]{:S(2)}) async-start(f32[8,256,128]{2,1,0:T(8,128)} %second_products.1), calls=%async_computation.2 | async-start | bytes 2097152 | tf_op jit(solution)/shard_map/second_products/all_to_all | solution.py:332
  89.0 15.6 %all-to-all-done.2.late_ref = f32[8,256,128]{2,1,0:T(8,128)S(1)} async-done(((f32[8,256,128]{2,1,0:T(8,128)}), f32[8,256,128]{2,1,0:T(8,128)S(1)}, u32[]{:S(2)}, u32[]{:S(2)}) %all-to-all-start.2) | async-done | bytes 1048608 | tf_op jit(solution)/shard_map/second_products/all_to_all | solution.py:332
  104.7 0.9 parts_to_owners.1
  105.6 14.0 %all_to_all.20.got_ref = f32[8,152,128]{2,1,0:T(8,128)S(1)} all-to-all(f32[8,152,128]{2,1,0:T(8,128)S(1)} %parts_to_owners.1), channel_id=1, replica_groups=mesh['row'=64,'col'=8] {'col'}, dimensions={0} | all-to-all | bytes 1245184 | tf_op jit(solution)/shard_map/parts_to_owners/all_to_all | solution.py:344
  119.6 2.0 %owned_results.1 = (f32[2,128,128]{2,1,0:T(8,128)}, f32[2,128,128]{2,1,0:T(8,128)}, f32[2,128,128]{2,1,0:T(8,128)}, f32[2,128,128]{2,1,0:T(8,128)}, f32[2,128,128]{2,1,0:T(8,128)}) custom-call(s32[8]{0:T(128)S(1)} %bitcast.37, f32[8,152,128]{2,1,0:T(8,128)S(1)} %all_to_all.20.got_ref), custom_call_target="tpu_custom_call" | custom-call | tf_op jit(solution)/shard_map/owned_results/owned_results/pallas_call | solution.py:348
  (20 shorter events, 0.2 us)
Async XLA Ops:
  2.2 0.7 copy-start.3
  2.9 17.9 %copy-start.1 = (bf16[8,128,336]{1,2,0:T(8,128)(2,1)S(1)}, bf16[8,128,336]{1,2,0:T(8,128)(2,1)}, u32[]{:S(2)}) copy-start(bf16[8,128,336]{1,2,0:T(8,128)(2,1)} %param.11) | copy-start | bytes 2064388
  2.9 17.9 %copy-start.2 = (bf16[8,128,336]{1,2,0:T(8,128)(2,1)S(1)}, bf16[8,128,336]{1,2,0:T(8,128)(2,1)}, u32[]{:S(2)}) copy-start(bf16[8,128,336]{1,2,0:T(8,128)(2,1)} %param.12) | copy-start | bytes 2064388
  2.9 17.9 %copy-start.4 = (s32[8]{0:T(128)S(1)}, s32[8]{0:T(128)}, u32[]{:S(2)}) copy-start(s32[8]{0:T(128)} %rank_ref.1) | copy-start | bytes 100
  4.4 30.4 %all-to-all-start = ((bf16[64,16,128]{2,1,0:T(8,128)(2,1)}), bf16[64,16,128]{2,1,0:T(8,128)(2,1)S(1)}, u32[]{:S(2)}, u32[]{:S(2)}) async-start(bf16[64,16,128]{2,1,0:T(8,128)(2,1)} %bitcast.12), calls=%async_computation | async-start | bytes 524288 | tf_op jit(solution)/shard_map/slices_out/all_to_all | solution.py:270
  22.2 0.9 copy-start.5
  36.7 45.8 %all-to-all-start.1 = ((bf16[64,8,1408]{2,1,0:T(8,128)(2,1)}), bf16[64,8,1408]{2,1,0:T(8,128)(2,1)S(1)}, u32[]{:S(2)}, u32[]{:S(2)}) async-start(bf16[64,8,1408]{2,1,0:T(8,128)(2,1)} %fusion), calls=%async_computation.1 | async-start | bytes 2883584 | tf_op jit(solution)/shard_map/tiles_asked_for/all_to_all | solution.py:316
  42.8 10.6 %collective-permute-start = (f32[2,2,136,128]{3,2,1,0:T(8,128)S(1)}, f32[2,2,136,128]{3,2,1,0:T(8,128)S(1)}, u32[]{:S(2)}, u32[]{:S(2)}) collective-permute-start(f32[2,2,136,128]{3,2,1,0:T(8,128)S(1)} %get-tuple-element.15), channel_id=1, source_target_pairs={{0,2},{1,3},{2,0},{3,1},{4,6},{5,7},{6,4},{7,5},{8,10},{9,11},{10,... | collective-permute-start | bytes 835592 | tf_op jit(solution)/shard_map/first_sum/ppermute | solution.py:233
  46.2 12.1 %collective-permute-start.2 = (f32[2,2,144,128]{3,2,1,0:T(8,128)S(1)}, f32[2,2,144,128]{3,2,1,0:T(8,128)S(1)}, u32[]{:S(2)}, u32[]{:S(2)}) collective-permute-start(f32[2,2,144,128]{3,2,1,0:T(8,128)S(1)} %get-tuple-element.17), channel_id=1, source_target_pairs={{0,6},{1,7},{2,4},{3,5},{4,2},{5,3},{6,0},{7,1},{8,14},{9,15},{10,... | collective-permute-start | bytes 884744 | tf_op jit(solution)/shard_map/first_sum/ppermute | solution.py:233
  53.4 29.1 %copy-start.6 = (bf16[8,128,384]{2,1,0:T(8,128)(2,1)S(1)}, bf16[8,128,384]{2,1,0:T(8,128)(2,1)}, u32[]{:S(2)}) copy-start(bf16[8,128,384]{2,1,0:T(8,128)(2,1)} %copy-done.5) | copy-start | bytes 2359300
  53.4 8.3 %collective-permute-start.1 = (f32[2,136,128]{2,1,0:T(8,128)S(1)}, f32[2,136,128]{2,1,0:T(8,128)S(1)}, u32[]{:S(2)}, u32[]{:S(2)}) collective-permute-start(f32[2,136,128]{2,1,0:T(8,128)S(1)} %slice_bitcast_fusion.2), channel_id=1, source_target_pairs={{0,6},{1,7},{2,4},{3,5},{4,2},{5,3},{6,0},{7,1},{8,14},{9,15},{10,... | collective-permute-start | bytes 417800 | tf_op jit(solution)/shard_map/first_sum/ppermute | solution.py:233
  58.3 7.0 %collective-permute-start.3 = (f32[2,144,128]{2,1,0:T(8,128)S(1)}, f32[2,144,128]{2,1,0:T(8,128)S(1)}, u32[]{:S(2)}, u32[]{:S(2)}) collective-permute-start(f32[2,144,128]{2,1,0:T(8,128)S(1)} %slice_bitcast_fusion), channel_id=1, source_target_pairs={{0,2},{1,3},{2,0},{3,1},{4,6},{5,7},{6,4},{7,5},{8,10},{9,11},{10,... | collective-permute-start | bytes 442376 | tf_op jit(solution)/shard_map/first_sum/ppermute | solution.py:233
  65.4 15.8 %collective-permute-start.4 = (f32[280,128]{1,0:T(8,128)S(1)}, f32[280,128]{1,0:T(8,128)S(1)}, u32[]{:S(2)}, u32[]{:S(2)}) collective-permute-start(f32[280,128]{1,0:T(8,128)S(1)} %pad_maximum_fusion.1), channel_id=1, source_target_pairs={{0,1},{1,0},{2,3},{3,2},{4,5},{5,4},{6,7},{7,6},{8,9},{9,8},{10,11... | collective-permute-start | bytes 430088 | tf_op jit(solution)/shard_map/first_sum/ppermute | solution.py:233
  84.6 20.1 %copy-start = (s32[8,1]{0,1:T(1,128)S(1)}, s32[8,1]{0,1:T(1,128)}, u32[]{:S(2)}) copy-start(s32[8,1]{0,1:T(1,128)} %param.15) | copy-start | bytes 100
  84.6 20.1 %all-to-all-start.2 = ((f32[8,256,128]{2,1,0:T(8,128)}), f32[8,256,128]{2,1,0:T(8,128)S(1)}, u32[]{:S(2)}, u32[]{:S(2)}) async-start(f32[8,256,128]{2,1,0:T(8,128)} %second_products.1), calls=%async_computation.2 | async-start | bytes 2097152 | tf_op jit(solution)/shard_map/second_products/all_to_all | solution.py:332

commit v3 on v2

--- a/solution.py
+++ b/solution.py
@@ -10,12 +10,13 @@
 TILES = 8
 PEERS = 64
 COLS = 8
+HOLDERS = PEERS // 2
 EACH = 10
-SLICED = EACH * PEERS // 2
+SLICED = EACH * HOLDERS
 SHARED = S - SLICED
-WIDE = (EACH + 1) * K
-BLOCK = 16
-HALF = K // 2
+LAST = 2 * EACH
+WIDE = (LAST + 1) * K
+BLOCK = 24
 LONG = 3 * K
 PART = K // COLS
 EARLY = TILES * PART
@@ -65,24 +66,25 @@
     return first, second
 
 
-def slices_kernel(cols_ref, kept_ref, slices_ref, rows, blocks):
-    lane = lax.broadcasted_iota(jnp.int32, (SHARED, K), 1)
-    wanted = jnp.zeros((SHARED, K), jnp.int32)
-    for t in range(TILES):
-        wanted = jnp.where(lane % HALF == t, cols_ref[t], wanted)
-    wanted = wanted.astype(jnp.float32)
-    blocks[...] = jnp.zeros_like(blocks)
+def slices_kernel(kept_ref, slices_ref, rows, ends, blocks):
+    wanted = kept_ref[2 * S : 2 * S + 16, :].astype(jnp.float32)
+    wanted = jnp.concatenate([wanted, wanted], axis=0)
     for which in range(2):
-        kept = kept_ref[which]
+        kept = kept_ref[which * S : (which + 1) * S, :]
         rows[which * SLICED : (which + 1) * SLICED, :] = kept[:SLICED].astype(jnp.float32)
-        ends = kept[SLICED:].astype(jnp.float32)
-        at = which * PEERS // 2 * BLOCK + EACH
-        blocks[pl.ds(at, SHARED, stride=2 * BLOCK), :] = jnp.where(lane < HALF, ends, wanted)
-        blocks[pl.ds(at + BLOCK, SHARED, stride=2 * BLOCK), :] = jnp.where(
-            lane < HALF, wanted, ends
-        )
-    for q in range(EACH):
-        blocks[pl.ds(q, PEERS, stride=BLOCK), :] = rows[pl.ds(q, PEERS, stride=EACH), :]
+        ends[which * SHARED : (which + 1) * SHARED, :] = kept[SLICED:].astype(jnp.float32)
+    for core in range(2):
+
+        def place(at, part):
+            blocks[pl.ds(core * BLOCK + at, HOLDERS, stride=2 * BLOCK), :] = part
+
+        for which in range(2):
+            for q in range(EACH):
+                place(which * EACH + q, rows[pl.ds(which * SLICED + q, HOLDERS, stride=EACH), :])
+        place(LAST, ends[...])
+        place(LAST + 1, wanted)
+        for at in range(LAST + 2, BLOCK):
+            place(at, jnp.zeros((HOLDERS, K), jnp.float32))
     slices_ref[...] = blocks[...].astype(jnp.bfloat16)
 
 
@@ -92,6 +94,7 @@
 
 
 def early_kernel(
+    owner_ref,
     rank_ref,
     kept_ref,
     x_ref,
@@ -106,8 +109,8 @@
     diagonals,
     gram,
 ):
-    left = kept_ref[0]
-    right_turned[...] = turned(kept_ref[1])
+    left = kept_ref[:S]
+    right_turned[...] = turned(kept_ref[S : 2 * S])
     gram[...] = tile_dot(left, left)
     row_at = lax.broadcasted_iota(jnp.int32, (K, K), 0)
     col_at = lax.broadcasted_iota(jnp.int32, (K, K), 1)
@@ -141,29 +144,25 @@
 
 
 def late_kernel(
-    got_ref, right_ref, y_ref, out_ref, rows, halves
+    got_ref, right_ref, y_ref, out_ref, rows, ends
 ):
-    for pair in range(PEERS // 2):
+    for pair in range(HOLDERS // 2):
         part = got_ref[16 * pair : 16 * pair + 16, :].astype(jnp.float32)
         for side in range(2):
-            peer = 2 * pair + side
+            holder = 2 * pair + side
             mine = part[8 * side : 8 * side + 8]
-            for q in range(EACH):
-                at = 8 * (peer * EACH + q)
-                rows[at : at + 8, :] = mine[:, q * K : (q + 1) * K]
-            halves[8 * peer : 8 * peer + 8, :] = mine[:, EACH * K :]
+            for which in range(2):
+                for q in range(EACH):
+                    at = 8 * (which * SLICED + holder * EACH + q)
+                    from_lane = (which * EACH + q) * K
+                    rows[at : at + 8, :] = mine[:, from_lane : from_lane + K]
+            ends[8 * holder : 8 * holder + 8, :] = mine[:, LAST * K :]
     right = right_ref[...]
     filler = jnp.zeros((LONG - S, K), jnp.bfloat16)
-    low = lax.broadcasted_iota(jnp.int32, (SHARED, K), 1) < HALF
 
     def panel_tile(t, which):
-        body = rows[pl.ds(which * SLICED * 8 + t, SLICED, stride=8), :]
-        at = which * PEERS * 4 + t
-        end = jnp.where(
-            low,
-            halves[pl.ds(at, SHARED, stride=16), :],
-            halves[pl.ds(at + 8, SHARED, stride=16), :],
-        )
+        body = rows[pl.ds(8 * which * SLICED + t, SLICED, stride=8), :]
+        end = ends[pl.ds(8 * which * SHARED + t, SHARED, stride=8), :]
         return jnp.concatenate(
             [body.astype(jnp.bfloat16), end.astype(jnp.bfloat16), filler], axis=0
         )
@@ -200,10 +199,17 @@
                 out_ref[column, there, :] = jnp.zeros((4 * PART, K), jnp.float32)
 
         out_ref[column, 8 * PART : 9 * PART, :] = gram
-        out_ref[column, 9 * PART :, :] = diagonal
-
-
-def final_kernel(owner_ref, got_ref, lo_ref, lc_ref, ln_ref, ro_ref, rc_ref):
+        out_ref[column, 9 * PART :, :] = jnp.zeros((8, K), jnp.float32)
+
+    here = lax.axis_index("col")
+    place = jnp.int32(0)
+    for t in range(TILES):
+        place = place + ((t < here) & (owner_ref[t] == owner_ref[here])).astype(jnp.int32)
+    row_at = lax.broadcasted_iota(jnp.int32, (8, K), 0)
+    out_ref[owner_ref[here], 9 * PART :, :] = jnp.where(row_at == place, diagonal, 0.0)
+
+
+def final_kernel(got_ref, lo_ref, lc_ref, ln_ref, ro_ref, rc_ref):
     row_at = lax.broadcasted_iota(jnp.int32, (K, K), 0)
     col_at = lax.broadcasted_iota(jnp.int32, (K, K), 1)
 
@@ -213,12 +219,15 @@
         )
 
     gram = whole(8)
-    for place, t in enumerate(owned_tiles(owner_ref, lax.axis_index("col"))):
+    diagonals = got_ref[0, 9 * PART :, :]
+    for c in range(1, COLS):
+        diagonals = diagonals + got_ref[c, 9 * PART :, :]
+    for place in range(2):
         part_left = whole(4 * place)
         mixed = whole(4 * place + 1)
         core = whole(4 * place + 2)
         part_right = whole(4 * place + 3)
-        diagonal = jnp.where(t >= 0, got_ref[jnp.maximum(t, 0), 9 * PART :, :][:1], 0.0)
+        diagonal = diagonals[place : place + 1]
         across = mixed.T
         lo_ref[place] = jnp.where(row_at <= col_at, mixed, across)
         ro_ref[place] = jnp.where(
@@ -254,19 +263,27 @@
     owners = owner[:, 0]
 
     with jax.named_scope("slices_out"):
-        kept = keep(jnp.stack([ut, vt]), panel_rank[0])
+        wanted = jnp.pad(tile_cols.astype(jnp.bfloat16), (0, K - TILES))
+        kept = jnp.concatenate(
+            [
+                keep(ut, panel_rank[0]),
+                keep(vt, panel_rank[0]),
+                jnp.broadcast_to(wanted, (16, K)),
+            ]
+        )
         slices = pl.pallas_call(
             slices_kernel,
-            in_specs=smem(1) + vmem(1),
+            in_specs=vmem(1),
             out_shape=jax.ShapeDtypeStruct((PEERS * BLOCK, K), jnp.bfloat16),
             scratch_shapes=[
                 pltpu.VMEM((2 * SLICED, K), jnp.float32),
+                pltpu.VMEM((2 * SHARED, K), jnp.float32),
                 pltpu.VMEM((PEERS * BLOCK, K), jnp.float32),
             ],
             compiler_params=params,
             cost_estimate=cost(1),
             name="slices_out",
-        )(tile_cols, kept)
+        )(kept)
         held = lax.all_to_all(slices.reshape(PEERS, BLOCK, K), "row", 0, 0)
         held = held.reshape(PEERS, BLOCK * K)
 
@@ -275,7 +292,7 @@
         second = jax.ShapeDtypeStruct((2, 2, SECOND, K), jnp.float32)
         *pieces, right_turned, y_turned = pl.pallas_call(
             early_kernel,
-            in_specs=smem(1) + vmem(3),
+            in_specs=smem(2) + vmem(3),
             out_shape=[
                 first,
                 first,
@@ -292,8 +309,9 @@
             compiler_params=params,
             cost_estimate=cost(4),
             name="first_products",
-        )(trail_rank, kept, xt, yt)
-        held, *_ = lax.optimization_barrier((held, *pieces))
+        )(owners, trail_rank, kept, xt, yt)
+
+    held, *_ = lax.optimization_barrier((held, *pieces))
 
     with jax.named_scope("first_sum"):
         first_sent, first_kept, second_sent, second_kept = pieces
@@ -305,16 +323,21 @@
         early_came = swapped(jnp.concatenate([first[1], second[1]]), 1)
 
     with jax.named_scope("tiles_asked_for"):
-        at = jnp.where(lax.axis_index("row") % 2 == 0, EACH * K + HALF, EACH * K)
-        asked = lax.dynamic_slice(held, (0, at), (PEERS, TILES)).astype(jnp.int32)
-        chosen = asked.reshape(PEERS * TILES, 1) == lax.broadcasted_iota(
-            jnp.int32, (PEERS * TILES, PEERS), 1
+        asked = held[:, WIDE : WIDE + TILES].reshape(HOLDERS, 2, TILES)
+        asked = jnp.where(lax.axis_index("row") % 2 == 0, asked[:, 0], asked[:, 1])
+        chosen = asked.astype(jnp.int32).reshape(HOLDERS * TILES, 1) == lax.broadcasted_iota(
+            jnp.int32, (HOLDERS * TILES, PEERS), 1
         )
         sent = jnp.dot(
             chosen.astype(jnp.bfloat16), held[:, :WIDE], preferred_element_type=jnp.float32
         ).astype(jnp.bfloat16)
-        got = lax.all_to_all(sent.reshape(PEERS, TILES, WIDE), "row", 0, 0)
-        got, early_came = lax.optimization_barrier((got, early_came))
+        same_core = [list(range(core, PEERS, 2)) for core in range(2)]
+        got = lax.all_to_all(
+            sent.reshape(HOLDERS, TILES, WIDE), "row", 0, 0, axis_index_groups=same_core
+        )
+        got, early_kept, early_came, owners = lax.optimization_barrier(
+            (got, early_kept, early_came, owners)
+        )
 
     with jax.named_scope("second_products"):
         late = pl.pallas_call(
@@ -322,13 +345,13 @@
             in_specs=vmem(3),
             out_shape=jax.ShapeDtypeStruct((COLS, 2 * K, K), jnp.float32),
             scratch_shapes=[
-                pltpu.VMEM((PEERS * EACH * TILES, K), jnp.float32),
-                pltpu.VMEM((PEERS * TILES, K), jnp.float32),
+                pltpu.VMEM((2 * SLICED * TILES, K), jnp.float32),
+                pltpu.VMEM((HOLDERS * TILES, K), jnp.float32),
             ],
             compiler_params=params,
             cost_estimate=cost(4),
             name="second_products",
-        )(got.reshape(PEERS * TILES, WIDE), right_turned, y_turned)
+        )(got.reshape(HOLDERS * TILES, WIDE), right_turned, y_turned)
         late = lax.all_to_all(late, "col", 0, 0)
 
     with jax.named_scope("parts_to_owners"):
@@ -347,11 +370,10 @@
         result = jax.ShapeDtypeStruct((2, K, K), jnp.float32)
         return pl.pallas_call(
             final_kernel,
-            in_specs=smem(1) + vmem(1),
             out_shape=(result,) * 5,
             compiler_params=params,
             name="owned_results",
-        )(owners, owned)
+        )(owned)
 
 
 def solution(mesh):

time: 122 us -> 119 us (0.975)
  the two profiles are of different devices: /device:TPU:24 before, /device:TPU:32 now
where the time goes in v3:
time: 119 us; the launch traced here: 118 us
  starting transfers between devices  41.3 us (35%)
  blocking collectives  34.5 us (29%)
  waiting for transfers between devices  30.3 us (25%)
  Pallas kernels  5.93 us (5%)
  other arithmetic  1.84 us (2%)
  matrix products  1.67 us (1%)
  between operations  1.56 us (1%)
    all_to_all x1, blocking collectives, per_device(): late = lax.all_to_all(late, 'col', 0, 0)  21.5 us
    ppermute x5, waiting for transfers between devices, swapped(): return lax.ppermute(block, 'col', [(c, c ^ away) for c in range(COLS)])  18.1 us
    ppermute x5, starting transfers between devices, swapped(): return lax.ppermute(block, 'col', [(c, c ^ away) for c in range(COLS)])  17.5 us
    all_to_all x1, starting transfers between devices, per_device(): held = lax.all_to_all(slices.reshape(PEERS, BLOCK, K), 'row', 0, 0)  16.3 us
    all_to_all x1, blocking collectives, per_device(): owned = lax.all_to_all(owned, 'col', 0, 0)  13 us
    all_to_all x1, waiting for transfers between devices, per_device(): held = lax.all_to_all(slices.reshape(PEERS, BLOCK, K), 'row', 0, 0)  12.3 us
    all_to_all x1, starting transfers between devices, per_device(): lax.all_to_all(sent.reshape(HOLDERS, TILES, WIDE), 'row', 0, 0, axis_inde...  7.48 us
  transfers between devices with their start and end apart: 7, of which 6 were waited for; matrix products, arithmetic and copies ran while one was open for 0% of the time, Pallas kernels for 1%

profile of v3, /device:TPU:32, one launch (start us, length us, event | category | flops | bytes accessed | tf_op | source)
XLA Modules:
  0.0 118.2 jit_solution(7575620375699342803)
XLA Ops:
  1.3 0.7 convert_element_type.19
  2.0 0.9 bitcast_select_fusion.1
  2.9 0.0 copy-start
  3.0 0.0 copy-start.1
  3.0 0.0 copy-start.2
  3.0 0.0 copy-start.3
  3.0 1.1 slices_out.1
  4.1 16.3 %all-to-all-start = ((bf16[64,24,128]{2,1,0:T(8,128)(2,1)}), bf16[64,24,128]{2,1,0:T(8,128)(2,1)S(1)}, u32[]{:S(2)}, u32[]{:S(2)}) async-start(bf16[64,24,128]{2,1,0:T(8,128)(2,1)} %bitcast.5), calls=%async_computation | async-start | bytes 786432 | tf_op jit(solution)/shard_map/slices_out/all_to_all | solution.py:287
  20.5 1.4 %first_products.1 = (f32[2,2,136,128]{3,2,1,0:T(8,128)S(1)}, f32[2,2,136,128]{3,2,1,0:T(8,128)S(1)}, f32[2,2,144,128]{3,2,1,0:T(8,128)S(1)}, f32[2,2,144,128]{3,...) custom-call(s32[8]{0:T(128)S(1)} %bitcast.45, s32[8]{0:T(128)S(1)} %copy-done.2, ...), custom_call_target="tpu_custom_call" | custom-call | flops 4000000000 | tf_op jit(solution)/shard_map/first_products/first_products/pallas_call | solution.py:293
  21.9 0.9 copy-done.4
  22.8 12.3 %all-to-all-done = bf16[64,24,128]{2,1,0:T(8,128)(2,1)S(1)} async-done(((bf16[64,24,128]{2,1,0:T(8,128)(2,1)}), bf16[64,24,128]{2,1,0:T(8,128)(2,1)S(1)}, u32[]{:S(2)}, u32[]{:S(2)}) %all-to-all-start) | async-done | bytes 393248 | tf_op jit(solution)/shard_map/slices_out/all_to_all | solution.py:287
  35.0 0.1 copy.15
  35.1 0.1 fusion.6
  35.2 0.1 reshape.45
  35.3 1.7 %fusion = bf16[32,8,2688]{2,1,0:T(8,128)(2,1)} fusion(bf16[64,3072]{1,0:T(8,128)(2,1)S(1)} %bitcast.49, s32[256]{0:T(256)S(1)} %reshape.45), kind=kOutput, calls=%fused_computation.1 | convolution fusion | flops 88784896 | bytes 1721344 | tf_op jit(solution)/shard_map/tiles_asked_for/dot_general | solution.py:331
  36.9 7.5 %all-to-all-start.1 = ((bf16[32,8,2688]{2,1,0:T(8,128)(2,1)}), bf16[32,8,2688]{2,1,0:T(8,128)(2,1)S(1)}, u32[]{:S(2)}, u32[]{:S(2)}) async-start(bf16[32,8,2688]{2,1,0:T(8,128)(2,1)} %fusion), calls=%async_computation.1 | async-start | bytes 2752512 | tf_op jit(solution)/shard_map/tiles_asked_for/all_to_all | solution.py:335
  44.4 3.4 %collective-permute-start = (f32[2,2,136,128]{3,2,1,0:T(8,128)S(1)}, f32[2,2,136,128]{3,2,1,0:T(8,128)S(1)}, u32[]{:S(2)}, u32[]{:S(2)}) collective-permute-start(f32[2,2,136,128]{3,2,1,0:T(8,128)S(1)} %get-tuple-element.16), channel_id=1, source_target_pairs={{0,2},{1,3},{2,0},{3,1},{4,6},{5,7},{6,4},{7,5},{8,10},{9,11},{10,... | collective-permute-start | bytes 835592 | tf_op jit(solution)/shard_map/first_sum/ppermute | solution.py:242
  47.8 4.0 %collective-permute-start.2 = (f32[2,2,144,128]{3,2,1,0:T(8,128)S(1)}, f32[2,2,144,128]{3,2,1,0:T(8,128)S(1)}, u32[]{:S(2)}, u32[]{:S(2)}) collective-permute-start(f32[2,2,144,128]{3,2,1,0:T(8,128)S(1)} %get-tuple-element.18), channel_id=1, source_target_pairs={{0,6},{1,7},{2,4},{3,5},{4,2},{5,3},{6,0},{7,1},{8,14},{9,15},{10,... | collective-permute-start | bytes 884744 | tf_op jit(solution)/shard_map/first_sum/ppermute | solution.py:242
  51.8 2.4 %collective-permute-done = f32[2,2,136,128]{3,2,1,0:T(8,128)S(1)} collective-permute-done((f32[2,2,136,128]{3,2,1,0:T(8,128)S(1)}, f32[2,2,136,128]{3,2,1,0:T(8,128)S(1)}, u32[]{:S(2)}, u32[]{:S(2)}) %collective-permute-start) | collective-permute-done | bytes 278560 | tf_op jit(solution)/shard_map/first_sum/ppermute | solution.py:242
  54.2 4.7 %collective-permute-start.1 = (f32[2,136,128]{2,1,0:T(8,128)S(1)}, f32[2,136,128]{2,1,0:T(8,128)S(1)}, u32[]{:S(2)}, u32[]{:S(2)}) collective-permute-start(f32[2,136,128]{2,1,0:T(8,128)S(1)} %slice_bitcast_fusion.2), channel_id=1, source_target_pairs={{0,6},{1,7},{2,4},{3,5},{4,2},{5,3},{6,0},{7,1},{8,14},{9,15},{10,... | collective-permute-start | bytes 417800 | tf_op jit(solution)/shard_map/first_sum/ppermute | solution.py:242
  58.9 0.4 collective-permute-done.2
  59.4 2.1 %collective-permute-start.3 = (f32[2,144,128]{2,1,0:T(8,128)S(1)}, f32[2,144,128]{2,1,0:T(8,128)S(1)}, u32[]{:S(2)}, u32[]{:S(2)}) collective-permute-start(f32[2,144,128]{2,1,0:T(8,128)S(1)} %slice_bitcast_fusion), channel_id=1, source_target_pairs={{0,2},{1,3},{2,0},{3,1},{4,6},{5,7},{6,4},{7,5},{8,10},{9,11},{10,... | collective-permute-start | bytes 442376 | tf_op jit(solution)/shard_map/first_sum/ppermute | solution.py:242
  61.5 0.9 collective-permute-done.1
  62.4 4.1 %collective-permute-done.3 = f32[2,144,128]{2,1,0:T(8,128)S(1)} collective-permute-done((f32[2,144,128]{2,1,0:T(8,128)S(1)}, f32[2,144,128]{2,1,0:T(8,128)S(1)}, u32[]{:S(2)}, u32[]{:S(2)}) %collective-permute-start.3) | collective-permute-done | bytes 147488 | tf_op jit(solution)/shard_map/first_sum/ppermute | solution.py:242
  66.6 3.4 %collective-permute-start.4 = (f32[280,128]{1,0:T(8,128)S(1)}, f32[280,128]{1,0:T(8,128)S(1)}, u32[]{:S(2)}, u32[]{:S(2)}) collective-permute-start(f32[280,128]{1,0:T(8,128)S(1)} %pad_maximum_fusion.2), channel_id=1, source_target_pairs={{0,1},{1,0},{2,3},{3,2},{4,5},{5,4},{6,7},{7,6},{8,9},{9,8},{10,11... | collective-permute-start | bytes 430088 | tf_op jit(solution)/shard_map/first_sum/ppermute | solution.py:242
  70.1 10.2 %collective-permute-done.4.came_ref = f32[280,128]{1,0:T(8,128)S(1)} collective-permute-done((f32[280,128]{1,0:T(8,128)S(1)}, f32[280,128]{1,0:T(8,128)S(1)}, u32[]{:S(2)}, u32[]{:S(2)}) %collective-permute-start.4) | collective-permute-done | bytes 143392 | tf_op jit(solution)/shard_map/first_sum/ppermute | solution.py:242
  80.3 0.0 all-to-all-done.1
  80.3 1.0 second_products.1
  81.3 21.5 %all_to_all.20.late_ref = f32[8,256,128]{2,1,0:T(8,128)S(1)} all-to-all(f32[8,256,128]{2,1,0:T(8,128)S(1)} %second_products.1), channel_id=1, replica_groups=mesh['row'=64,'col'=8] {'col'}, dimensions={0} | all-to-all | bytes 2097152 | tf_op jit(solution)/shard_map/second_products/all_to_all | solution.py:355
  102.8 0.9 parts_to_owners.1
  103.7 13.0 %all_to_all.21.got_ref = f32[8,152,128]{2,1,0:T(8,128)S(1)} all-to-all(f32[8,152,128]{2,1,0:T(8,128)S(1)} %parts_to_owners.1), channel_id=1, replica_groups=mesh['row'=64,'col'=8] {'col'}, dimensions={0} | all-to-all | bytes 1245184 | tf_op jit(solution)/shard_map/parts_to_owners/all_to_all | solution.py:367
  116.7 1.5 %owned_results.1 = (f32[2,128,128]{2,1,0:T(8,128)}, f32[2,128,128]{2,1,0:T(8,128)}, f32[2,128,128]{2,1,0:T(8,128)}, f32[2,128,128]{2,1,0:T(8,128)}, f32[2,128,128]{2,1,0:T(8,128)}) custom-call(f32[8,152,128]{2,1,0:T(8,128)S(1)} %all_to_all.21.got_ref), custom_call_target="tpu_custom_call" | custom-call | tf_op jit(solution)/shard_map/owned_results/owned_results/pallas_call | solution.py:371
  (22 shorter events, 0.2 us)
Async XLA Ops:
  2.9 17.5 %copy-start = (bf16[8,128,336]{1,2,0:T(8,128)(2,1)S(1)}, bf16[8,128,336]{1,2,0:T(8,128)(2,1)}, u32[]{:S(2)}) copy-start(bf16[8,128,336]{1,2,0:T(8,128)(2,1)} %param.11) | copy-start | bytes 2064388
  3.0 17.5 %copy-start.1 = (bf16[8,128,336]{1,2,0:T(8,128)(2,1)S(1)}, bf16[8,128,336]{1,2,0:T(8,128)(2,1)}, u32[]{:S(2)}) copy-start(bf16[8,128,336]{1,2,0:T(8,128)(2,1)} %param.12) | copy-start | bytes 2064388
  3.0 17.5 %copy-start.2 = (s32[8]{0:T(128)S(1)}, s32[8]{0:T(128)}, u32[]{:S(2)}) copy-start(s32[8]{0:T(128)} %rank_ref.1) | copy-start | bytes 100
  3.0 17.5 %copy-start.3 = (s32[8,1]{0,1:T(1,128)S(1)}, s32[8,1]{0,1:T(1,128)}, u32[]{:S(2)}) copy-start(s32[8,1]{0,1:T(1,128)} %param.15) | copy-start | bytes 100
  4.1 30.9 %all-to-all-start = ((bf16[64,24,128]{2,1,0:T(8,128)(2,1)}), bf16[64,24,128]{2,1,0:T(8,128)(2,1)S(1)}, u32[]{:S(2)}, u32[]{:S(2)}) async-start(bf16[64,24,128]{2,1,0:T(8,128)(2,1)} %bitcast.5), calls=%async_computation | async-start | bytes 786432 | tf_op jit(solution)/shard_map/slices_out/all_to_all | solution.py:287
  21.9 0.9 copy-start.4
  36.9 43.4 %all-to-all-start.1 = ((bf16[32,8,2688]{2,1,0:T(8,128)(2,1)}), bf16[32,8,2688]{2,1,0:T(8,128)(2,1)S(1)}, u32[]{:S(2)}, u32[]{:S(2)}) async-start(bf16[32,8,2688]{2,1,0:T(8,128)(2,1)} %fusion), calls=%async_computation.1 | async-start | bytes 2752512 | tf_op jit(solution)/shard_map/tiles_asked_for/all_to_all | solution.py:335
  44.4 9.8 %collective-permute-start = (f32[2,2,136,128]{3,2,1,0:T(8,128)S(1)}, f32[2,2,136,128]{3,2,1,0:T(8,128)S(1)}, u32[]{:S(2)}, u32[]{:S(2)}) collective-permute-start(f32[2,2,136,128]{3,2,1,0:T(8,128)S(1)} %get-tuple-element.16), channel_id=1, source_target_pairs={{0,2},{1,3},{2,0},{3,1},{4,6},{5,7},{6,4},{7,5},{8,10},{9,11},{10,... | collective-permute-start | bytes 835592 | tf_op jit(solution)/shard_map/first_sum/ppermute | solution.py:242
  47.8 11.5 %collective-permute-start.2 = (f32[2,2,144,128]{3,2,1,0:T(8,128)S(1)}, f32[2,2,144,128]{3,2,1,0:T(8,128)S(1)}, u32[]{:S(2)}, u32[]{:S(2)}) collective-permute-start(f32[2,2,144,128]{3,2,1,0:T(8,128)S(1)} %get-tuple-element.18), channel_id=1, source_target_pairs={{0,6},{1,7},{2,4},{3,5},{4,2},{5,3},{6,0},{7,1},{8,14},{9,15},{10,... | collective-permute-start | bytes 884744 | tf_op jit(solution)/shard_map/first_sum/ppermute | solution.py:242
  54.2 8.2 %collective-permute-start.1 = (f32[2,136,128]{2,1,0:T(8,128)S(1)}, f32[2,136,128]{2,1,0:T(8,128)S(1)}, u32[]{:S(2)}, u32[]{:S(2)}) collective-permute-start(f32[2,136,128]{2,1,0:T(8,128)S(1)} %slice_bitcast_fusion.2), channel_id=1, source_target_pairs={{0,6},{1,7},{2,4},{3,5},{4,2},{5,3},{6,0},{7,1},{8,14},{9,15},{10,... | collective-permute-start | bytes 417800 | tf_op jit(solution)/shard_map/first_sum/ppermute | solution.py:242
  59.4 20.9 %copy-start.5 = (bf16[8,128,384]{2,1,0:T(8,128)(2,1)S(1)}, bf16[8,128,384]{2,1,0:T(8,128)(2,1)}, u32[]{:S(2)}) copy-start(bf16[8,128,384]{2,1,0:T(8,128)(2,1)} %copy-done.4) | copy-start | bytes 2359300
  59.4 7.2 %collective-permute-start.3 = (f32[2,144,128]{2,1,0:T(8,128)S(1)}, f32[2,144,128]{2,1,0:T(8,128)S(1)}, u32[]{:S(2)}, u32[]{:S(2)}) collective-permute-start(f32[2,144,128]{2,1,0:T(8,128)S(1)} %slice_bitcast_fusion), channel_id=1, source_target_pairs={{0,2},{1,3},{2,0},{3,1},{4,6},{5,7},{6,4},{7,5},{8,10},{9,11},{10,... | collective-permute-start | bytes 442376 | tf_op jit(solution)/shard_map/first_sum/ppermute | solution.py:242
  66.6 13.6 %collective-permute-start.4 = (f32[280,128]{1,0:T(8,128)S(1)}, f32[280,128]{1,0:T(8,128)S(1)}, u32[]{:S(2)}, u32[]{:S(2)}) collective-permute-start(f32[280,128]{1,0:T(8,128)S(1)} %pad_maximum_fusion.2), channel_id=1, source_target_pairs={{0,1},{1,0},{2,3},{3,2},{4,5},{5,4},{6,7},{7,6},{8,9},{9,8},{10,11... | collective-permute-start | bytes 430088 | tf_op jit(solution)/shard_map/first_sum/ppermute | solution.py:242

commit v4 on v3

--- a/solution.py
+++ b/solution.py
@@ -28,6 +28,7 @@
     for base in (0, FIRST)
     for at in range(base, base + EARLY, 2 * PART)
 ]
+SPARE = 16
 VMEM = 32 * 1024 * 1024
 
 
@@ -85,7 +86,7 @@
         place(LAST + 1, wanted)
         for at in range(LAST + 2, BLOCK):
             place(at, jnp.zeros((HOLDERS, K), jnp.float32))
-    slices_ref[...] = blocks[...].astype(jnp.bfloat16)
+    slices_ref[...] = blocks[: PEERS * BLOCK, :].astype(jnp.bfloat16)
 
 
 def turned(block):
@@ -276,9 +277,9 @@
             in_specs=vmem(1),
             out_shape=jax.ShapeDtypeStruct((PEERS * BLOCK, K), jnp.bfloat16),
             scratch_shapes=[
-                pltpu.VMEM((2 * SLICED, K), jnp.float32),
+                pltpu.VMEM((2 * SLICED + SPARE, K), jnp.float32),
                 pltpu.VMEM((2 * SHARED, K), jnp.float32),
-                pltpu.VMEM((PEERS * BLOCK, K), jnp.float32),
+                pltpu.VMEM((PEERS * BLOCK + 4 * SPARE, K), jnp.float32),
             ],
             compiler_params=params,
             cost_estimate=cost(1),
@@ -345,8 +346,8 @@
             in_specs=vmem(3),
             out_shape=jax.ShapeDtypeStruct((COLS, 2 * K, K), jnp.float32),
             scratch_shapes=[
-                pltpu.VMEM((2 * SLICED * TILES, K), jnp.float32),
-                pltpu.VMEM((HOLDERS * TILES, K), jnp.float32),
+                pltpu.VMEM((2 * SLICED * TILES + SPARE, K), jnp.float32),
+                pltpu.VMEM((HOLDERS * TILES + SPARE, K), jnp.float32),
             ],
             compiler_params=params,
             cost_estimate=cost(4),

time: 119 us -> 119 us (level)
  no operation moved by 1% of the time
where the time goes in v4:
time: 119 us; the launch traced here: 118 us
  starting transfers between devices  41.3 us (35%)
  blocking collectives  34.6 us (29%)
  waiting for transfers between devices  30.3 us (25%)
  Pallas kernels  5.93 us (5%)
  other arithmetic  1.84 us (2%)
  matrix products  1.67 us (1%)
  between operations  1.56 us (1%)
    all_to_all x1, blocking collectives, per_device(): late = lax.all_to_all(late, 'col', 0, 0)  21.5 us
    ppermute x5, waiting for transfers between devices, swapped(): return lax.ppermute(block, 'col', [(c, c ^ away) for c in range(COLS)])  18.1 us
    ppermute x5, starting transfers between devices, swapped(): return lax.ppermute(block, 'col', [(c, c ^ away) for c in range(COLS)])  17.5 us
    all_to_all x1, starting transfers between devices, per_device(): held = lax.all_to_all(slices.reshape(PEERS, BLOCK, K), 'row', 0, 0)  16.3 us
    all_to_all x1, blocking collectives, per_device(): owned = lax.all_to_all(owned, 'col', 0, 0)  13 us
    all_to_all x1, waiting for transfers between devices, per_device(): held = lax.all_to_all(slices.reshape(PEERS, BLOCK, K), 'row', 0, 0)  12.3 us
    all_to_all x1, starting transfers between devices, per_device(): lax.all_to_all(sent.reshape(HOLDERS, TILES, WIDE), 'row', 0, 0, axis_inde...  7.49 us
  transfers between devices with their start and end apart: 7, of which 6 were waited for; matrix products, arithmetic and copies ran while one was open for 0% of the time, Pallas kernels for 1%

profile of v4, /device:TPU:32, one launch (start us, length us, event | category | flops | bytes accessed | tf_op | source)
XLA Modules:
  0.0 118.3 jit_solution(9064599258341788322)
XLA Ops:
  1.3 0.7 convert_element_type.19
  2.0 0.9 bitcast_select_fusion.1
  2.9 0.0 copy-start
  3.0 0.0 copy-start.1
  3.0 0.0 copy-start.2
  3.0 0.0 copy-start.3
  3.0 1.1 slices_out.1
  4.1 16.3 %all-to-all-start = ((bf16[64,24,128]{2,1,0:T(8,128)(2,1)}), bf16[64,24,128]{2,1,0:T(8,128)(2,1)S(1)}, u32[]{:S(2)}, u32[]{:S(2)}) async-start(bf16[64,24,128]{2,1,0:T(8,128)(2,1)} %bitcast.5), calls=%async_computation | async-start | bytes 786432 | tf_op jit(solution)/shard_map/slices_out/all_to_all | solution.py:288
  20.5 1.4 %first_products.1 = (f32[2,2,136,128]{3,2,1,0:T(8,128)S(1)}, f32[2,2,136,128]{3,2,1,0:T(8,128)S(1)}, f32[2,2,144,128]{3,2,1,0:T(8,128)S(1)}, f32[2,2,144,128]{3,...) custom-call(s32[8]{0:T(128)S(1)} %bitcast.45, s32[8]{0:T(128)S(1)} %copy-done.2, ...), custom_call_target="tpu_custom_call" | custom-call | flops 4000000000 | tf_op jit(solution)/shard_map/first_products/first_products/pallas_call | solution.py:294
  21.9 0.9 copy-done.4
  22.8 12.3 %all-to-all-done = bf16[64,24,128]{2,1,0:T(8,128)(2,1)S(1)} async-done(((bf16[64,24,128]{2,1,0:T(8,128)(2,1)}), bf16[64,24,128]{2,1,0:T(8,128)(2,1)S(1)}, u32[]{:S(2)}, u32[]{:S(2)}) %all-to-all-start) | async-done | bytes 393248 | tf_op jit(solution)/shard_map/slices_out/all_to_all | solution.py:288
  35.0 0.1 copy.15
  35.1 0.1 fusion.6
  35.2 0.1 reshape.45
  35.3 1.7 %fusion = bf16[32,8,2688]{2,1,0:T(8,128)(2,1)} fusion(bf16[64,3072]{1,0:T(8,128)(2,1)S(1)} %bitcast.49, s32[256]{0:T(256)S(1)} %reshape.45), kind=kOutput, calls=%fused_computation.1 | convolution fusion | flops 88784896 | bytes 1721344 | tf_op jit(solution)/shard_map/tiles_asked_for/dot_general | solution.py:332
  36.9 7.5 %all-to-all-start.1 = ((bf16[32,8,2688]{2,1,0:T(8,128)(2,1)}), bf16[32,8,2688]{2,1,0:T(8,128)(2,1)S(1)}, u32[]{:S(2)}, u32[]{:S(2)}) async-start(bf16[32,8,2688]{2,1,0:T(8,128)(2,1)} %fusion), calls=%async_computation.1 | async-start | bytes 2752512 | tf_op jit(solution)/shard_map/tiles_asked_for/all_to_all | solution.py:336
  44.4 3.4 %collective-permute-start = (f32[2,2,136,128]{3,2,1,0:T(8,128)S(1)}, f32[2,2,136,128]{3,2,1,0:T(8,128)S(1)}, u32[]{:S(2)}, u32[]{:S(2)}) collective-permute-start(f32[2,2,136,128]{3,2,1,0:T(8,128)S(1)} %get-tuple-element.16), channel_id=1, source_target_pairs={{0,2},{1,3},{2,0},{3,1},{4,6},{5,7},{6,4},{7,5},{8,10},{9,11},{10,... | collective-permute-start | bytes 835592 | tf_op jit(solution)/shard_map/first_sum/ppermute | solution.py:243
  47.8 4.0 %collective-permute-start.2 = (f32[2,2,144,128]{3,2,1,0:T(8,128)S(1)}, f32[2,2,144,128]{3,2,1,0:T(8,128)S(1)}, u32[]{:S(2)}, u32[]{:S(2)}) collective-permute-start(f32[2,2,144,128]{3,2,1,0:T(8,128)S(1)} %get-tuple-element.18), channel_id=1, source_target_pairs={{0,6},{1,7},{2,4},{3,5},{4,2},{5,3},{6,0},{7,1},{8,14},{9,15},{10,... | collective-permute-start | bytes 884744 | tf_op jit(solution)/shard_map/first_sum/ppermute | solution.py:243
  51.8 2.4 %collective-permute-done = f32[2,2,136,128]{3,2,1,0:T(8,128)S(1)} collective-permute-done((f32[2,2,136,128]{3,2,1,0:T(8,128)S(1)}, f32[2,2,136,128]{3,2,1,0:T(8,128)S(1)}, u32[]{:S(2)}, u32[]{:S(2)}) %collective-permute-start) | collective-permute-done | bytes 278560 | tf_op jit(solution)/shard_map/first_sum/ppermute | solution.py:243
  54.2 4.7 %collective-permute-start.1 = (f32[2,136,128]{2,1,0:T(8,128)S(1)}, f32[2,136,128]{2,1,0:T(8,128)S(1)}, u32[]{:S(2)}, u32[]{:S(2)}) collective-permute-start(f32[2,136,128]{2,1,0:T(8,128)S(1)} %slice_bitcast_fusion.2), channel_id=1, source_target_pairs={{0,6},{1,7},{2,4},{3,5},{4,2},{5,3},{6,0},{7,1},{8,14},{9,15},{10,... | collective-permute-start | bytes 417800 | tf_op jit(solution)/shard_map/first_sum/ppermute | solution.py:243
  58.9 0.4 collective-permute-done.2
  59.4 2.1 %collective-permute-start.3 = (f32[2,144,128]{2,1,0:T(8,128)S(1)}, f32[2,144,128]{2,1,0:T(8,128)S(1)}, u32[]{:S(2)}, u32[]{:S(2)}) collective-permute-start(f32[2,144,128]{2,1,0:T(8,128)S(1)} %slice_bitcast_fusion), channel_id=1, source_target_pairs={{0,2},{1,3},{2,0},{3,1},{4,6},{5,7},{6,4},{7,5},{8,10},{9,11},{10,... | collective-permute-start | bytes 442376 | tf_op jit(solution)/shard_map/first_sum/ppermute | solution.py:243
  61.5 0.9 collective-permute-done.1
  62.4 4.1 %collective-permute-done.3 = f32[2,144,128]{2,1,0:T(8,128)S(1)} collective-permute-done((f32[2,144,128]{2,1,0:T(8,128)S(1)}, f32[2,144,128]{2,1,0:T(8,128)S(1)}, u32[]{:S(2)}, u32[]{:S(2)}) %collective-permute-start.3) | collective-permute-done | bytes 147488 | tf_op jit(solution)/shard_map/first_sum/ppermute | solution.py:243
  66.7 3.4 %collective-permute-start.4 = (f32[280,128]{1,0:T(8,128)S(1)}, f32[280,128]{1,0:T(8,128)S(1)}, u32[]{:S(2)}, u32[]{:S(2)}) collective-permute-start(f32[280,128]{1,0:T(8,128)S(1)} %pad_maximum_fusion.2), channel_id=1, source_target_pairs={{0,1},{1,0},{2,3},{3,2},{4,5},{5,4},{6,7},{7,6},{8,9},{9,8},{10,11... | collective-permute-start | bytes 430088 | tf_op jit(solution)/shard_map/first_sum/ppermute | solution.py:243
  70.0 10.2 %collective-permute-done.4.came_ref = f32[280,128]{1,0:T(8,128)S(1)} collective-permute-done((f32[280,128]{1,0:T(8,128)S(1)}, f32[280,128]{1,0:T(8,128)S(1)}, u32[]{:S(2)}, u32[]{:S(2)}) %collective-permute-start.4) | collective-permute-done | bytes 143392 | tf_op jit(solution)/shard_map/first_sum/ppermute | solution.py:243
  80.3 0.0 all-to-all-done.1
  80.3 1.0 second_products.1
  81.3 21.5 %all_to_all.20.late_ref = f32[8,256,128]{2,1,0:T(8,128)S(1)} all-to-all(f32[8,256,128]{2,1,0:T(8,128)S(1)} %second_products.1), channel_id=1, replica_groups=mesh['row'=64,'col'=8] {'col'}, dimensions={0} | all-to-all | bytes 2097152 | tf_op jit(solution)/shard_map/second_products/all_to_all | solution.py:356
  102.9 0.9 parts_to_owners.1
  103.8 13.0 %all_to_all.21.got_ref = f32[8,152,128]{2,1,0:T(8,128)S(1)} all-to-all(f32[8,152,128]{2,1,0:T(8,128)S(1)} %parts_to_owners.1), channel_id=1, replica_groups=mesh['row'=64,'col'=8] {'col'}, dimensions={0} | all-to-all | bytes 1245184 | tf_op jit(solution)/shard_map/parts_to_owners/all_to_all | solution.py:368
  116.8 1.5 %owned_results.1 = (f32[2,128,128]{2,1,0:T(8,128)}, f32[2,128,128]{2,1,0:T(8,128)}, f32[2,128,128]{2,1,0:T(8,128)}, f32[2,128,128]{2,1,0:T(8,128)}, f32[2,128,128]{2,1,0:T(8,128)}) custom-call(f32[8,152,128]{2,1,0:T(8,128)S(1)} %all_to_all.21.got_ref), custom_call_target="tpu_custom_call" | custom-call | tf_op jit(solution)/shard_map/owned_results/owned_results/pallas_call | solution.py:372
  (22 shorter events, 0.2 us)
Async XLA Ops:
  2.9 17.5 %copy-start = (bf16[8,128,336]{1,2,0:T(8,128)(2,1)S(1)}, bf16[8,128,336]{1,2,0:T(8,128)(2,1)}, u32[]{:S(2)}) copy-start(bf16[8,128,336]{1,2,0:T(8,128)(2,1)} %param.11) | copy-start | bytes 2064388
  3.0 17.5 %copy-start.1 = (bf16[8,128,336]{1,2,0:T(8,128)(2,1)S(1)}, bf16[8,128,336]{1,2,0:T(8,128)(2,1)}, u32[]{:S(2)}) copy-start(bf16[8,128,336]{1,2,0:T(8,128)(2,1)} %param.12) | copy-start | bytes 2064388
  3.0 17.5 %copy-start.2 = (s32[8]{0:T(128)S(1)}, s32[8]{0:T(128)}, u32[]{:S(2)}) copy-start(s32[8]{0:T(128)} %rank_ref.1) | copy-start | bytes 100
  3.0 17.5 %copy-start.3 = (s32[8,1]{0,1:T(1,128)S(1)}, s32[8,1]{0,1:T(1,128)}, u32[]{:S(2)}) copy-start(s32[8,1]{0,1:T(1,128)} %param.15) | copy-start | bytes 100
  4.1 30.9 %all-to-all-start = ((bf16[64,24,128]{2,1,0:T(8,128)(2,1)}), bf16[64,24,128]{2,1,0:T(8,128)(2,1)S(1)}, u32[]{:S(2)}, u32[]{:S(2)}) async-start(bf16[64,24,128]{2,1,0:T(8,128)(2,1)} %bitcast.5), calls=%async_computation | async-start | bytes 786432 | tf_op jit(solution)/shard_map/slices_out/all_to_all | solution.py:288
  21.9 0.9 copy-start.4
  36.9 43.4 %all-to-all-start.1 = ((bf16[32,8,2688]{2,1,0:T(8,128)(2,1)}), bf16[32,8,2688]{2,1,0:T(8,128)(2,1)S(1)}, u32[]{:S(2)}, u32[]{:S(2)}) async-start(bf16[32,8,2688]{2,1,0:T(8,128)(2,1)} %fusion), calls=%async_computation.1 | async-start | bytes 2752512 | tf_op jit(solution)/shard_map/tiles_asked_for/all_to_all | solution.py:336
  44.4 9.8 %collective-permute-start = (f32[2,2,136,128]{3,2,1,0:T(8,128)S(1)}, f32[2,2,136,128]{3,2,1,0:T(8,128)S(1)}, u32[]{:S(2)}, u32[]{:S(2)}) collective-permute-start(f32[2,2,136,128]{3,2,1,0:T(8,128)S(1)} %get-tuple-element.16), channel_id=1, source_target_pairs={{0,2},{1,3},{2,0},{3,1},{4,6},{5,7},{6,4},{7,5},{8,10},{9,11},{10,... | collective-permute-start | bytes 835592 | tf_op jit(solution)/shard_map/first_sum/ppermute | solution.py:243
  47.8 11.5 %collective-permute-start.2 = (f32[2,2,144,128]{3,2,1,0:T(8,128)S(1)}, f32[2,2,144,128]{3,2,1,0:T(8,128)S(1)}, u32[]{:S(2)}, u32[]{:S(2)}) collective-permute-start(f32[2,2,144,128]{3,2,1,0:T(8,128)S(1)} %get-tuple-element.18), channel_id=1, source_target_pairs={{0,6},{1,7},{2,4},{3,5},{4,2},{5,3},{6,0},{7,1},{8,14},{9,15},{10,... | collective-permute-start | bytes 884744 | tf_op jit(solution)/shard_map/first_sum/ppermute | solution.py:243
  54.2 8.2 %collective-permute-start.1 = (f32[2,136,128]{2,1,0:T(8,128)S(1)}, f32[2,136,128]{2,1,0:T(8,128)S(1)}, u32[]{:S(2)}, u32[]{:S(2)}) collective-permute-start(f32[2,136,128]{2,1,0:T(8,128)S(1)} %slice_bitcast_fusion.2), channel_id=1, source_target_pairs={{0,6},{1,7},{2,4},{3,5},{4,2},{5,3},{6,0},{7,1},{8,14},{9,15},{10,... | collective-permute-start | bytes 417800 | tf_op jit(solution)/shard_map/first_sum/ppermute | solution.py:243
  59.4 20.9 %copy-start.5 = (bf16[8,128,384]{2,1,0:T(8,128)(2,1)S(1)}, bf16[8,128,384]{2,1,0:T(8,128)(2,1)}, u32[]{:S(2)}) copy-start(bf16[8,128,384]{2,1,0:T(8,128)(2,1)} %copy-done.4) | copy-start | bytes 2359300
  59.4 7.2 %collective-permute-start.3 = (f32[2,144,128]{2,1,0:T(8,128)S(1)}, f32[2,144,128]{2,1,0:T(8,128)S(1)}, u32[]{:S(2)}, u32[]{:S(2)}) collective-permute-start(f32[2,144,128]{2,1,0:T(8,128)S(1)} %slice_bitcast_fusion), channel_id=1, source_target_pairs={{0,2},{1,3},{2,0},{3,1},{4,6},{5,7},{6,4},{7,5},{8,10},{9,11},{10,... | collective-permute-start | bytes 442376 | tf_op jit(solution)/shard_map/first_sum/ppermute | solution.py:243
  66.7 13.6 %collective-permute-start.4 = (f32[280,128]{1,0:T(8,128)S(1)}, f32[280,128]{1,0:T(8,128)S(1)}, u32[]{:S(2)}, u32[]{:S(2)}) collective-permute-start(f32[280,128]{1,0:T(8,128)S(1)} %pad_maximum_fusion.2), channel_id=1, source_target_pairs={{0,1},{1,0},{2,3},{3,2},{4,5},{5,4},{6,7},{7,6},{8,9},{9,8},{10,11... | collective-permute-start | bytes 430088 | tf_op jit(solution)/shard_map/first_sum/ppermute | solution.py:243

commit v5 on v4

--- a/solution.py
+++ b/solution.py
@@ -18,6 +18,7 @@
 WIDE = (LAST + 1) * K
 BLOCK = 24
 LONG = 3 * K
+RUNS = [(0, 4), (4, 8), (8, 12), (12, 16), (16, 21)]
 PART = K // COLS
 EARLY = TILES * PART
 FIRST = EARLY + 8
@@ -144,6 +145,37 @@
         ref[at, across, EARLY:, :] = gram[pl.ds(start, PART), :]
 
 
+def gather_kernel(held_ref, out_ref, blocks, sent, gone):
+    blocks[: PEERS * BLOCK, :] = held_ref[...].astype(jnp.float32)
+    asked = jnp.where(
+        lax.axis_index("row") % 2 == 0,
+        blocks[pl.ds(LAST + 1, HOLDERS, stride=2 * BLOCK), :],
+        blocks[pl.ds(LAST + 1 + BLOCK, HOLDERS, stride=2 * BLOCK), :],
+    )
+    count = HOLDERS * TILES
+    holder = lax.broadcasted_iota(jnp.int32, (count, HOLDERS), 1)
+    spread = lax.broadcasted_iota(jnp.int32, (count, HOLDERS), 0) // TILES == holder
+    asked = plain_dot(spread.astype(jnp.bfloat16), asked.astype(jnp.bfloat16))
+    tile = lax.broadcasted_iota(jnp.int32, (count, K), 0) % TILES
+    lane = lax.broadcasted_iota(jnp.int32, (count, K), 1)
+    asked = jnp.sum(jnp.where(lane == tile, asked, 0.0), axis=1, keepdims=True)
+    peer = lax.broadcasted_iota(jnp.int32, (count, PEERS), 1)
+    chosen = (asked.astype(jnp.int32) == peer).astype(jnp.bfloat16)
+    copies = []
+    for run, (start, stop) in enumerate(RUNS):
+        parts = [
+            blocks[pl.ds(at, PEERS, stride=BLOCK), :].astype(jnp.bfloat16)
+            for at in range(start, stop)
+        ]
+        lanes = slice(start * K, stop * K)
+        sent[:, lanes] = plain_dot(chosen, jnp.concatenate(parts, axis=1)).astype(jnp.bfloat16)
+        copy = pltpu.make_async_copy(sent.at[:, lanes], out_ref.at[:, lanes], gone.at[run])
+        copy.start()
+        copies.append(copy)
+    for copy in copies:
+        copy.wait()
+
+
 def late_kernel(
     got_ref, right_ref, y_ref, out_ref, rows, ends
 ):
@@ -177,16 +209,16 @@
             out_ref[c, base + PART : base + 2 * PART, :] = part_right[c * PART : (c + 1) * PART]
 
 
-def route_kernel(owner_ref, kept_ref, came_ref, late_ref, out_ref, sums):
+def route_kernel(owner_ref, early_ref, late_ref, out_ref, sums):
     for t in range(TILES):
         base = 2 * t * PART
-        sums[t, : 2 * PART, :] = kept_ref[EARLY_AT[t], :] + came_ref[EARLY_AT[t], :]
+        sums[t, : 2 * PART, :] = early_ref[EARLY_AT[t], :]
         total = late_ref[0, base : base + 2 * PART, :]
         for c in range(1, COLS):
             total = total + late_ref[c, base : base + 2 * PART, :]
         sums[t, 2 * PART :, :] = total
-    diagonal = kept_ref[EARLY:FIRST, :] + came_ref[EARLY:FIRST, :]
-    gram = kept_ref[FIRST + EARLY :, :] + came_ref[FIRST + EARLY :, :]
+    diagonal = early_ref[EARLY:FIRST, :]
+    gram = early_ref[FIRST + EARLY :, :]
     for column in range(COLS):
         for place, t in enumerate(owned_tiles(owner_ref, column)):
             there = slice(4 * place * PART, 4 * (place + 1) * PART)
@@ -286,7 +318,7 @@
             name="slices_out",
         )(kept)
         held = lax.all_to_all(slices.reshape(PEERS, BLOCK, K), "row", 0, 0)
-        held = held.reshape(PEERS, BLOCK * K)
+        held = held.reshape(PEERS * BLOCK, K)
 
     with jax.named_scope("first_products"):
         first = jax.ShapeDtypeStruct((2, 2, FIRST, K), jnp.float32)
@@ -324,21 +356,25 @@
         early_came = swapped(jnp.concatenate([first[1], second[1]]), 1)
 
     with jax.named_scope("tiles_asked_for"):
-        asked = held[:, WIDE : WIDE + TILES].reshape(HOLDERS, 2, TILES)
-        asked = jnp.where(lax.axis_index("row") % 2 == 0, asked[:, 0], asked[:, 1])
-        chosen = asked.astype(jnp.int32).reshape(HOLDERS * TILES, 1) == lax.broadcasted_iota(
-            jnp.int32, (HOLDERS * TILES, PEERS), 1
-        )
-        sent = jnp.dot(
-            chosen.astype(jnp.bfloat16), held[:, :WIDE], preferred_element_type=jnp.float32
-        ).astype(jnp.bfloat16)
+        sent = pl.pallas_call(
+            gather_kernel,
+            in_specs=vmem(1),
+            out_specs=pl.BlockSpec(memory_space=pl.ANY),
+            out_shape=jax.ShapeDtypeStruct((HOLDERS * TILES, WIDE), jnp.bfloat16),
+            scratch_shapes=[
+                pltpu.VMEM((PEERS * BLOCK + 4 * SPARE, K), jnp.float32),
+                pltpu.VMEM((HOLDERS * TILES, WIDE), jnp.bfloat16),
+                pltpu.SemaphoreType.DMA((len(RUNS),)),
+            ],
+            compiler_params=params,
+            cost_estimate=cost(1),
+            name="tiles_asked_for",
+        )(held)
         same_core = [list(range(core, PEERS, 2)) for core in range(2)]
         got = lax.all_to_all(
             sent.reshape(HOLDERS, TILES, WIDE), "row", 0, 0, axis_index_groups=same_core
         )
-        got, early_kept, early_came, owners = lax.optimization_barrier(
-            (got, early_kept, early_came, owners)
-        )
+        got, early, owners = lax.optimization_barrier((got, early_kept + early_came, owners))
 
     with jax.named_scope("second_products"):
         late = pl.pallas_call(
@@ -358,13 +394,13 @@
     with jax.named_scope("parts_to_owners"):
         owned = pl.pallas_call(
             route_kernel,
-            in_specs=smem(1) + vmem(3),
+            in_specs=smem(1) + vmem(2),
             out_shape=jax.ShapeDtypeStruct((COLS, OWNED, K), jnp.float32),
             scratch_shapes=[pltpu.VMEM((TILES, 4 * PART, K), jnp.float32)],
             compiler_params=params,
             cost_estimate=cost(1),
             name="parts_to_owners",
-        )(owners, early_kept, early_came, late)
+        )(owners, early, late)
         owned = lax.all_to_all(owned, "col", 0, 0)
 
     with jax.named_scope("owned_results"):

time: 119 us -> 119 us (level)
  matrix products: 1.67 us -> 0 us
  Pallas kernels: 5.93 us -> 7.56 us
    dot_general x1 -> x0, matrix products: 1.67 us -> none  [per_device(): jnp.dot(chosen.astype(jnp.bfloat16), held[:, :WIDE], preferred_element_ty...]
    pallas_call x1 -> x2, Pallas kernels: 0.93 us -> 2.54 us  [the longest x1 1.62 us: per_device(): pl.pallas_call(gather_kernel, in_specs=vmem(1), out_specs=pl.BlockSpec(me...]
where the time goes in v5:
time: 119 us; the launch traced here: 118 us
  starting transfers between devices  41.3 us (35%)
  blocking collectives  34.5 us (29%)
  waiting for transfers between devices  30.4 us (26%)
  Pallas kernels  7.56 us (6%)
  other arithmetic  1.76 us (1%)
  between operations  1.54 us (1%)
    all_to_all x1, blocking collectives, per_device(): late = lax.all_to_all(late, 'col', 0, 0)  21.5 us
    ppermute x5, waiting for transfers between devices, swapped(): return lax.ppermute(block, 'col', [(c, c ^ away) for c in range(COLS)])  18.1 us
    ppermute x5, starting transfers between devices, swapped(): return lax.ppermute(block, 'col', [(c, c ^ away) for c in range(COLS)])  17.5 us
    all_to_all x1, starting transfers between devices, per_device(): held = lax.all_to_all(slices.reshape(PEERS, BLOCK, K), 'row', 0, 0)  16.3 us
    all_to_all x1, blocking collectives, per_device(): owned = lax.all_to_all(owned, 'col', 0, 0)  13 us
    all_to_all x1, waiting for transfers between devices, per_device(): held = lax.all_to_all(slices.reshape(PEERS, BLOCK, K), 'row', 0, 0)  12.3 us
    all_to_all x1, starting transfers between devices, per_device(): lax.all_to_all(sent.reshape(HOLDERS, TILES, WIDE), 'row', 0, 0, axis_inde...  7.49 us
  transfers between devices with their start and end apart: 7, of which 6 were waited for; matrix products, arithmetic and copies ran while one was open for 0% of the time, Pallas kernels for 1%

profile of v5, /device:TPU:32, one launch (start us, length us, event | category | flops | bytes accessed | tf_op | source)
XLA Modules:
  0.0 118.0 jit_solution(1004162714863375740)
XLA Ops:
  1.3 0.7 convert_element_type.5
  2.0 0.9 bitcast_select_fusion.1
  2.9 0.0 copy-start
  3.0 0.0 copy-start.1
  3.0 0.0 copy-start.2
  3.0 0.0 copy-start.3
  3.0 1.1 slices_out.1
  4.1 16.3 %all-to-all-start = ((bf16[64,24,128]{2,1,0:T(8,128)(2,1)}), bf16[64,24,128]{2,1,0:T(8,128)(2,1)S(1)}, u32[]{:S(2)}, u32[]{:S(2)}) async-start(bf16[64,24,128]{2,1,0:T(8,128)(2,1)} %bitcast.5), calls=%async_computation | async-start | bytes 786432 | tf_op jit(solution)/shard_map/slices_out/all_to_all | solution.py:320
  20.4 0.0 copy-done
  20.4 0.0 copy-done.1
  20.4 0.0 copy-done.2
  20.4 1.4 %first_products.1 = (f32[2,2,136,128]{3,2,1,0:T(8,128)S(1)}, f32[2,2,136,128]{3,2,1,0:T(8,128)S(1)}, f32[2,2,144,128]{3,2,1,0:T(8,128)S(1)}, f32[2,2,144,128]{3,...) custom-call(s32[8]{0:T(128)S(1)} %bitcast.41, s32[8]{0:T(128)S(1)} %copy-done.2, ...), custom_call_target="tpu_custom_call" | custom-call | flops 4000000000 | tf_op jit(solution)/shard_map/first_products/first_products/pallas_call | solution.py:326
  21.9 0.9 copy-done.4
  22.7 12.3 %all-to-all-done = bf16[64,24,128]{2,1,0:T(8,128)(2,1)S(1)} async-done(((bf16[64,24,128]{2,1,0:T(8,128)(2,1)}), bf16[64,24,128]{2,1,0:T(8,128)(2,1)S(1)}, u32[]{:S(2)}, u32[]{:S(2)}) %all-to-all-start) | async-done | bytes 393248 | tf_op jit(solution)/shard_map/slices_out/all_to_all | solution.py:320
  35.0 1.6 %tiles_asked_for.1 = bf16[256,2688]{1,0:T(8,128)(2,1)} custom-call(bf16[1536,128]{1,0:T(8,128)(2,1)S(1)} %bitcast.38), custom_call_target="tpu_custom_call" | custom-call | flops 1000000000 | tf_op jit(solution)/shard_map/tiles_asked_for/tiles_asked_for/pallas_call | solution.py:359
  36.6 7.5 %all-to-all-start.1 = ((bf16[32,8,2688]{2,1,0:T(8,128)(2,1)}), bf16[32,8,2688]{2,1,0:T(8,128)(2,1)S(1)}, u32[]{:S(2)}, u32[]{:S(2)}) async-start(bf16[32,8,2688]{2,1,0:T(8,128)(2,1)} %bitcast.10), calls=%async_computation.1 | async-start | bytes 2752512 | tf_op jit(solution)/shard_map/tiles_asked_for/all_to_all | solution.py:374
  44.1 3.4 %collective-permute-start = (f32[2,2,136,128]{3,2,1,0:T(8,128)S(1)}, f32[2,2,136,128]{3,2,1,0:T(8,128)S(1)}, u32[]{:S(2)}, u32[]{:S(2)}) collective-permute-start(f32[2,2,136,128]{3,2,1,0:T(8,128)S(1)} %get-tuple-element.15), channel_id=1, source_target_pairs={{0,2},{1,3},{2,0},{3,1},{4,6},{5,7},{6,4},{7,5},{8,10},{9,11},{10,... | collective-permute-start | bytes 835592 | tf_op jit(solution)/shard_map/first_sum/ppermute | solution.py:275
  47.5 4.0 %collective-permute-start.2 = (f32[2,2,144,128]{3,2,1,0:T(8,128)S(1)}, f32[2,2,144,128]{3,2,1,0:T(8,128)S(1)}, u32[]{:S(2)}, u32[]{:S(2)}) collective-permute-start(f32[2,2,144,128]{3,2,1,0:T(8,128)S(1)} %get-tuple-element.17), channel_id=1, source_target_pairs={{0,6},{1,7},{2,4},{3,5},{4,2},{5,3},{6,0},{7,1},{8,14},{9,15},{10,... | collective-permute-start | bytes 884744 | tf_op jit(solution)/shard_map/first_sum/ppermute | solution.py:275
  51.6 2.4 %collective-permute-done = f32[2,2,136,128]{3,2,1,0:T(8,128)S(1)} collective-permute-done((f32[2,2,136,128]{3,2,1,0:T(8,128)S(1)}, f32[2,2,136,128]{3,2,1,0:T(8,128)S(1)}, u32[]{:S(2)}, u32[]{:S(2)}) %collective-permute-start) | collective-permute-done | bytes 278560 | tf_op jit(solution)/shard_map/first_sum/ppermute | solution.py:275
  54.0 4.7 %collective-permute-start.1 = (f32[2,136,128]{2,1,0:T(8,128)S(1)}, f32[2,136,128]{2,1,0:T(8,128)S(1)}, u32[]{:S(2)}, u32[]{:S(2)}) collective-permute-start(f32[2,136,128]{2,1,0:T(8,128)S(1)} %slice_bitcast_fusion.2), channel_id=1, source_target_pairs={{0,6},{1,7},{2,4},{3,5},{4,2},{5,3},{6,0},{7,1},{8,14},{9,15},{10,... | collective-permute-start | bytes 417800 | tf_op jit(solution)/shard_map/first_sum/ppermute | solution.py:275
  58.6 0.4 collective-permute-done.2
  59.1 2.1 %collective-permute-start.3 = (f32[2,144,128]{2,1,0:T(8,128)S(1)}, f32[2,144,128]{2,1,0:T(8,128)S(1)}, u32[]{:S(2)}, u32[]{:S(2)}) collective-permute-start(f32[2,144,128]{2,1,0:T(8,128)S(1)} %slice_bitcast_fusion), channel_id=1, source_target_pairs={{0,2},{1,3},{2,0},{3,1},{4,6},{5,7},{6,4},{7,5},{8,10},{9,11},{10,... | collective-permute-start | bytes 442376 | tf_op jit(solution)/shard_map/first_sum/ppermute | solution.py:275
  61.2 0.9 collective-permute-done.1
  62.2 4.1 %collective-permute-done.3 = f32[2,144,128]{2,1,0:T(8,128)S(1)} collective-permute-done((f32[2,144,128]{2,1,0:T(8,128)S(1)}, f32[2,144,128]{2,1,0:T(8,128)S(1)}, u32[]{:S(2)}, u32[]{:S(2)}) %collective-permute-start.3) | collective-permute-done | bytes 147488 | tf_op jit(solution)/shard_map/first_sum/ppermute | solution.py:275
  66.4 3.4 %collective-permute-start.4 = (f32[280,128]{1,0:T(8,128)S(1)}, f32[280,128]{1,0:T(8,128)S(1)}, u32[]{:S(2)}, u32[]{:S(2)}) collective-permute-start(f32[280,128]{1,0:T(8,128)S(1)} %pad_maximum_fusion.1), channel_id=1, source_target_pairs={{0,1},{1,0},{2,3},{3,2},{4,5},{5,4},{6,7},{7,6},{8,9},{9,8},{10,11... | collective-permute-start | bytes 430088 | tf_op jit(solution)/shard_map/first_sum/ppermute | solution.py:275
  69.8 10.2 %collective-permute-done.4 = f32[280,128]{1,0:T(8,128)S(1)} collective-permute-done((f32[280,128]{1,0:T(8,128)S(1)}, f32[280,128]{1,0:T(8,128)S(1)}, u32[]{:S(2)}, u32[]{:S(2)}) %collective-permute-start.4) | collective-permute-done | bytes 143392 | tf_op jit(solution)/shard_map/first_sum/ppermute | solution.py:275
  80.0 0.0 all-to-all-done.1
  80.0 1.1 second_products.1
  81.1 21.5 %all_to_all.20.late_ref = f32[8,256,128]{2,1,0:T(8,128)S(1)} all-to-all(f32[8,256,128]{2,1,0:T(8,128)S(1)} %second_products.1), channel_id=1, replica_groups=mesh['row'=64,'col'=8] {'col'}, dimensions={0} | all-to-all | bytes 2097152 | tf_op jit(solution)/shard_map/second_products/all_to_all | solution.py:392
  102.6 0.9 parts_to_owners.1
  103.5 13.0 %all_to_all.21.got_ref = f32[8,152,128]{2,1,0:T(8,128)S(1)} all-to-all(f32[8,152,128]{2,1,0:T(8,128)S(1)} %parts_to_owners.1), channel_id=1, replica_groups=mesh['row'=64,'col'=8] {'col'}, dimensions={0} | all-to-all | bytes 1245184 | tf_op jit(solution)/shard_map/parts_to_owners/all_to_all | solution.py:404
  116.5 1.5 %owned_results.1 = (f32[2,128,128]{2,1,0:T(8,128)}, f32[2,128,128]{2,1,0:T(8,128)}, f32[2,128,128]{2,1,0:T(8,128)}, f32[2,128,128]{2,1,0:T(8,128)}, f32[2,128,128]{2,1,0:T(8,128)}) custom-call(f32[8,152,128]{2,1,0:T(8,128)S(1)} %all_to_all.21.got_ref), custom_call_target="tpu_custom_call" | custom-call | tf_op jit(solution)/shard_map/owned_results/owned_results/pallas_call | solution.py:408
  (18 shorter events, 0.2 us)
Async XLA Ops:
  2.9 17.5 %copy-start = (bf16[8,128,336]{1,2,0:T(8,128)(2,1)S(1)}, bf16[8,128,336]{1,2,0:T(8,128)(2,1)}, u32[]{:S(2)}) copy-start(bf16[8,128,336]{1,2,0:T(8,128)(2,1)} %param.11) | copy-start | bytes 2064388
  3.0 17.5 %copy-start.1 = (bf16[8,128,336]{1,2,0:T(8,128)(2,1)S(1)}, bf16[8,128,336]{1,2,0:T(8,128)(2,1)}, u32[]{:S(2)}) copy-start(bf16[8,128,336]{1,2,0:T(8,128)(2,1)} %param.12) | copy-start | bytes 2064388
  3.0 17.5 %copy-start.2 = (s32[8]{0:T(128)S(1)}, s32[8]{0:T(128)}, u32[]{:S(2)}) copy-start(s32[8]{0:T(128)} %rank_ref.1) | copy-start | bytes 100
  3.0 17.5 %copy-start.3 = (s32[8,1]{0,1:T(1,128)S(1)}, s32[8,1]{0,1:T(1,128)}, u32[]{:S(2)}) copy-start(s32[8,1]{0,1:T(1,128)} %param.15) | copy-start | bytes 100
  4.1 30.9 %all-to-all-start = ((bf16[64,24,128]{2,1,0:T(8,128)(2,1)}), bf16[64,24,128]{2,1,0:T(8,128)(2,1)S(1)}, u32[]{:S(2)}, u32[]{:S(2)}) async-start(bf16[64,24,128]{2,1,0:T(8,128)(2,1)} %bitcast.5), calls=%async_computation | async-start | bytes 786432 | tf_op jit(solution)/shard_map/slices_out/all_to_all | solution.py:320
  21.8 0.9 copy-start.4
  36.6 43.4 %all-to-all-start.1 = ((bf16[32,8,2688]{2,1,0:T(8,128)(2,1)}), bf16[32,8,2688]{2,1,0:T(8,128)(2,1)S(1)}, u32[]{:S(2)}, u32[]{:S(2)}) async-start(bf16[32,8,2688]{2,1,0:T(8,128)(2,1)} %bitcast.10), calls=%async_computation.1 | async-start | bytes 2752512 | tf_op jit(solution)/shard_map/tiles_asked_for/all_to_all | solution.py:374
  44.1 9.8 %collective-permute-start = (f32[2,2,136,128]{3,2,1,0:T(8,128)S(1)}, f32[2,2,136,128]{3,2,1,0:T(8,128)S(1)}, u32[]{:S(2)}, u32[]{:S(2)}) collective-permute-start(f32[2,2,136,128]{3,2,1,0:T(8,128)S(1)} %get-tuple-element.15), channel_id=1, source_target_pairs={{0,2},{1,3},{2,0},{3,1},{4,6},{5,7},{6,4},{7,5},{8,10},{9,11},{10,... | collective-permute-start | bytes 835592 | tf_op jit(solution)/shard_map/first_sum/ppermute | solution.py:275
  47.5 11.5 %collective-permute-start.2 = (f32[2,2,144,128]{3,2,1,0:T(8,128)S(1)}, f32[2,2,144,128]{3,2,1,0:T(8,128)S(1)}, u32[]{:S(2)}, u32[]{:S(2)}) collective-permute-start(f32[2,2,144,128]{3,2,1,0:T(8,128)S(1)} %get-tuple-element.17), channel_id=1, source_target_pairs={{0,6},{1,7},{2,4},{3,5},{4,2},{5,3},{6,0},{7,1},{8,14},{9,15},{10,... | collective-permute-start | bytes 884744 | tf_op jit(solution)/shard_map/first_sum/ppermute | solution.py:275
  54.0 8.2 %collective-permute-start.1 = (f32[2,136,128]{2,1,0:T(8,128)S(1)}, f32[2,136,128]{2,1,0:T(8,128)S(1)}, u32[]{:S(2)}, u32[]{:S(2)}) collective-permute-start(f32[2,136,128]{2,1,0:T(8,128)S(1)} %slice_bitcast_fusion.2), channel_id=1, source_target_pairs={{0,6},{1,7},{2,4},{3,5},{4,2},{5,3},{6,0},{7,1},{8,14},{9,15},{10,... | collective-permute-start | bytes 417800 | tf_op jit(solution)/shard_map/first_sum/ppermute | solution.py:275
  59.1 20.9 %copy-start.5 = (bf16[8,128,384]{2,1,0:T(8,128)(2,1)S(1)}, bf16[8,128,384]{2,1,0:T(8,128)(2,1)}, u32[]{:S(2)}) copy-start(bf16[8,128,384]{2,1,0:T(8,128)(2,1)} %copy-done.4) | copy-start | bytes 2359300
  59.1 7.2 %collective-permute-start.3 = (f32[2,144,128]{2,1,0:T(8,128)S(1)}, f32[2,144,128]{2,1,0:T(8,128)S(1)}, u32[]{:S(2)}, u32[]{:S(2)}) collective-permute-start(f32[2,144,128]{2,1,0:T(8,128)S(1)} %slice_bitcast_fusion), channel_id=1, source_target_pairs={{0,2},{1,3},{2,0},{3,1},{4,6},{5,7},{6,4},{7,5},{8,10},{9,11},{10,... | collective-permute-start | bytes 442376 | tf_op jit(solution)/shard_map/first_sum/ppermute | solution.py:275
  66.4 13.6 %collective-permute-start.4 = (f32[280,128]{1,0:T(8,128)S(1)}, f32[280,128]{1,0:T(8,128)S(1)}, u32[]{:S(2)}, u32[]{:S(2)}) collective-permute-start(f32[280,128]{1,0:T(8,128)S(1)} %pad_maximum_fusion.1), channel_id=1, source_target_pairs={{0,1},{1,0},{2,3},{3,2},{4,5},{5,4},{6,7},{7,6},{8,9},{9,8},{10,11... | collective-permute-start | bytes 430088 | tf_op jit(solution)/shard_map/first_sum/ppermute | solution.py:275
